TPU v7x, 32 devices: a whole 2x2x4 slice. The times are simulated.
32 devices in a mesh: dp: 8 (over z, x), tensor: 4 (over y, core).
Axes of the slice: x: 2, y: 2, z: 4, core: 2. Of those that a mesh axis runs over, the one named last changes fastest.
Arguments:
- tokens: bfloat16 [12608, 768], P(('dp', 'tensor')), may hold values from -6 to 6
- ln1_gain: bfloat16 [768], P(('dp', 'tensor')), may hold values from 0.5 to 1.5
- ln1_shift: bfloat16 [768], P(('dp', 'tensor')), may hold values from -1.5 to 1.5
- qkv_weight: bfloat16 [768, 3, 768], P('dp', None, 'tensor'), may hold values from -0.3125 to 0.3125
- qv_bias: bfloat16 [2, 768], P(None, ('dp', 'tensor')), may hold values from -1.5 to 1.5
- out_weight: bfloat16 [768, 768], P('tensor', 'dp'), may hold values from -0.875 to 0.875
- out_bias: bfloat16 [768], P(('dp', 'tensor')), may hold values from -1.5 to 1.5
- ln2_gain: bfloat16 [768], P(('dp', 'tensor')), may hold values from 0.5 to 1.5
- ln2_shift: bfloat16 [768], P(('dp', 'tensor')), may hold values from -1.5 to 1.5
- router_weight: bfloat16 [768, 8], P(('dp', 'tensor')), may hold values from -0.15625 to 0.15625
- expert_in: bfloat16 [8, 768, 3072], P(None, 'dp', 'tensor'), may hold values from -0.21875 to 0.21875
- expert_in_bias: bfloat16 [8, 3072], P(None, ('dp', 'tensor')), may hold values from -1.5 to 1.5
- expert_out: bfloat16 [8, 3072, 768], P(None, 'tensor', 'dp'), may hold values from -0.625 to 0.625
- expert_out_bias: bfloat16 [8, 768], P(None, ('dp', 'tensor')), may hold values from -1 to 1
- expert_ids: int32 [12608, 2], P('dp'), may hold values from 0 to 7, as said below
- expert_slots: int32 [12608, 2], P('dp'), may hold values from -1 to 629, as said below
- cotangent: bfloat16 [12608, 768], P(('dp', 'tensor')), may hold values from -6 to 6
Outputs:
- output: bfloat16 [12608, 768], P(('dp', 'tensor'))
- tokens_grad: float32 [12608, 768], P(('dp', 'tensor'))
- ln1_gain_grad: float32 [768], P(('dp', 'tensor'))
- ln1_shift_grad: float32 [768], P(('dp', 'tensor'))
- qkv_weight_grad: float32 [768, 3, 768], P('dp', None, 'tensor')
- qv_bias_grad: float32 [2, 768], P(None, ('dp', 'tensor'))
- out_weight_grad: float32 [768, 768], P('tensor', 'dp')
- out_bias_grad: float32 [768], P(('dp', 'tensor'))
- ln2_gain_grad: float32 [768], P(('dp', 'tensor'))
- ln2_shift_grad: float32 [768], P(('dp', 'tensor'))
- router_weight_grad: float32 [768, 8], P(('dp', 'tensor'))
- expert_in_grad: float32 [8, 768, 3072], P(None, 'dp', 'tensor')
- expert_in_bias_grad: float32 [8, 3072], P(None, ('dp', 'tensor'))
- expert_out_grad: float32 [8, 3072, 768], P(None, 'tensor', 'dp')
- expert_out_bias_grad: float32 [8, 768], P(None, ('dp', 'tensor'))
Inputs may be any that keep to these rules, and one draw needn't show every extreme that they name: `expert_ids`: each token names two different experts. `expert_slots`: within each group of 1576 tokens an expert's slots are taken from 0 upward, first by the first choices in token order, then by the second choices in token order; a choice that finds all 630 slots taken is dropped (-1).
All inputs are finite; a program needn't handle non-finite values.
Results may differ from a plain program's by a relative error of at most 0.02.
Values may be sent and summed in bfloat16 or wider, within the bound.
A program may use at most 256 MiB of HBM per device.

v0:
```python
import jax
import jax.numpy as jnp
from jax import lax
from jax.sharding import PartitionSpec as P

HEAD_DIM = 64
TOP = 2
SEQ = 197
CAP = 630


eps_norm = 1e-06
highest = lax.Precision.HIGHEST


def normalize(row_data, gain_vec, shift_vec):
    row_mean = jnp.mean(row_data, axis=-1, keepdims=True)
    centred = row_data - row_mean
    inv_std = lax.rsqrt(jnp.mean(centred * centred, axis=-1, keepdims=True) + eps_norm)
    unit_rows = centred * inv_std
    return (unit_rows * gain_vec + shift_vec, unit_rows, inv_std)


def norm_back(grad_out, unit_rows, inv_std, gain_vec):
    scaled = grad_out * gain_vec
    centred = scaled - jnp.mean(scaled, axis=-1, keepdims=True)
    grad_rows = inv_std * (
        centred - unit_rows * jnp.mean(scaled * unit_rows, axis=-1, keepdims=True)
    )
    return (grad_rows, jnp.sum(grad_out * unit_rows, axis=0), jnp.sum(grad_out, axis=0))


def body(
    tokens,
    ln1_gain,
    ln1_shift,
    qkv_weight,
    qv_bias,
    out_weight,
    out_bias,
    ln2_gain,
    ln2_shift,
    router_weight,
    expert_in,
    expert_in_bias,
    expert_out,
    expert_out_bias,
    expert_ids,
    expert_slots,
    cotangent,
):
    tensor_count = lax.axis_size("tensor")
    tensor_pos = lax.axis_index("tensor")
    rows_own = tokens.shape[0]
    model_width = tokens.shape[1]
    group_rows = rows_own * tensor_count
    own_start = tensor_pos * rows_own
    experts = expert_in.shape[0]
    qkv_gathered, proj_gathered, up_gathered, down_gathered = (
        lax.all_gather(qkv_weight, "dp", axis=0, tiled=True),
        lax.all_gather(out_weight, "dp", axis=1, tiled=True),
        lax.all_gather(expert_in, "dp", axis=1, tiled=True),
        lax.all_gather(expert_out, "dp", axis=2, tiled=True),
    )
    gathered_small = (
        lax.all_gather(ln1_gain, ("dp", "tensor"), axis=0, tiled=True),
        lax.all_gather(ln1_shift, ("dp", "tensor"), axis=0, tiled=True),
        lax.all_gather(ln2_gain, ("dp", "tensor"), axis=0, tiled=True),
        lax.all_gather(ln2_shift, ("dp", "tensor"), axis=0, tiled=True),
        lax.all_gather(qv_bias, ("dp", "tensor"), axis=1, tiled=True),
        lax.all_gather(out_bias, ("dp", "tensor"), axis=0, tiled=True),
        lax.all_gather(router_weight, ("dp", "tensor"), axis=0, tiled=True),
        lax.all_gather(expert_in_bias, ("dp", "tensor"), axis=1, tiled=True),
        lax.all_gather(expert_out_bias, ("dp", "tensor"), axis=1, tiled=True),
    )
    (
        gain_first,
        shift_first,
        gain_second,
        shift_second,
        bias_pair,
        bias_out,
        router_full,
        up_bias,
        down_bias,
    ) = [entry.astype(jnp.float32) for entry in gathered_small]
    router_low = gathered_small[6]
    head_cols = qkv_gathered.shape[2]
    ff_cols = up_gathered.shape[2]
    heads_here = head_cols // HEAD_DIM
    images = group_rows // SEQ
    shape_four = (images, SEQ, heads_here, HEAD_DIM)
    score_scale = HEAD_DIM ** (-0.5)
    bias_pair_own = lax.dynamic_slice_in_dim(bias_pair, tensor_pos * head_cols, head_cols, 1)
    up_bias_own = lax.dynamic_slice_in_dim(up_bias, tensor_pos * ff_cols, ff_cols, 1)
    inputs_f = tokens.astype(jnp.float32)
    first_own, unit_first, inv_first = normalize(inputs_f, gain_first, shift_first)
    first_norm = lax.all_gather(first_own.astype(jnp.bfloat16), "tensor", axis=0, tiled=True)
    projected = jnp.dot(
        first_norm,
        qkv_gathered.reshape(model_width, 3 * head_cols),
        preferred_element_type=jnp.float32,
    ).reshape(group_rows, 3, head_cols)
    queries = (projected[:, 0] + bias_pair_own[0]).astype(jnp.bfloat16).reshape(shape_four)
    keys_all = projected[:, 1].astype(jnp.bfloat16).reshape(shape_four)
    values_all = (projected[:, 2] + bias_pair_own[1]).astype(jnp.bfloat16).reshape(shape_four)
    scores = (
        jnp.einsum("bqhd,bkhd->bhqk", queries, keys_all, preferred_element_type=jnp.float32)
        * score_scale
    )
    row_max = jnp.max(scores, axis=-1, keepdims=True)
    log_total = row_max + jnp.log(jnp.sum(jnp.exp(scores - row_max), axis=-1, keepdims=True))
    attn_weights = jnp.exp(scores - log_total)
    mixed_rows = (
        jnp.einsum(
            "bhqk,bkhd->bqhd",
            attn_weights.astype(jnp.bfloat16),
            values_all,
            preferred_element_type=jnp.float32,
        )
        .reshape(group_rows, head_cols)
        .astype(jnp.bfloat16)
    )
    branch_own = (
        lax.psum_scatter(
            jnp.dot(mixed_rows, proj_gathered, preferred_element_type=jnp.float32).astype(
                jnp.bfloat16
            ),
            "tensor",
            scatter_dimension=0,
            tiled=True,
        ).astype(jnp.float32)
        + bias_out
    )
    hidden_rows = inputs_f + branch_own
    second_own, unit_second, inv_second = normalize(hidden_rows, gain_second, shift_second)
    second_low = second_own.astype(jnp.bfloat16)
    second_norm = lax.all_gather(second_low, "tensor", axis=0, tiled=True)
    router_logits = jnp.dot(second_norm, router_low, preferred_element_type=jnp.float32)
    router_probs = jax.nn.softmax(router_logits, axis=-1)
    labels = jnp.arange(experts, dtype=jnp.int32)
    onehot = (expert_ids[:, :, None] == labels).astype(jnp.float32)
    kept_mask = expert_slots >= 0
    kept_float = kept_mask.astype(jnp.float32)
    gate_vals = jnp.sum(onehot * router_probs[:, None, :], axis=-1) * kept_float
    spare_slot = experts * CAP
    slot_index = jnp.where(kept_mask, expert_ids * CAP + expert_slots, spare_slot)
    slot_list = slot_index.reshape(-1)
    dispatched = (
        jnp.zeros((spare_slot + 1, model_width), jnp.bfloat16)
        .at[slot_list]
        .set(jnp.repeat(second_norm, TOP, axis=0))[:spare_slot]
        .reshape(experts, CAP, model_width)
    )
    preact = (
        jnp.einsum("ecd,edf->ecf", dispatched, up_gathered, preferred_element_type=jnp.float32)
        + up_bias_own[:, None, :]
    )
    activated = jax.nn.gelu(preact, approximate=False).astype(jnp.bfloat16)
    expert_part = jnp.einsum(
        "ecf,efd->ecd", activated, down_gathered, preferred_element_type=jnp.float32
    ).reshape(spare_slot, model_width)
    part_padded = jnp.concatenate([expert_part, jnp.zeros((1, model_width), jnp.float32)], axis=0)
    picks = slot_index
    moe_own = lax.psum_scatter(
        jnp.sum(gate_vals[:, :, None] * part_padded[picks], axis=1).astype(jnp.bfloat16),
        "tensor",
        scatter_dimension=0,
        tiled=True,
    ).astype(jnp.float32)
    onehot_own = lax.dynamic_slice_in_dim(onehot, own_start, rows_own, 0)
    kept_own = lax.dynamic_slice_in_dim(kept_float, own_start, rows_own, 0)
    gates_own = lax.dynamic_slice_in_dim(gate_vals, own_start, rows_own, 0)
    probs_own = lax.dynamic_slice_in_dim(router_probs, own_start, rows_own, 0)
    route_own = onehot_own * kept_own[:, :, None]
    bias_term = jnp.einsum(
        "tke,ed->td", gates_own[:, :, None] * route_own, down_bias, precision=highest
    )
    final_rows = hidden_rows + moe_own + bias_term
    qkv_used, proj_used, up_used, down_used = (
        qkv_gathered,
        proj_gathered,
        up_gathered,
        down_gathered,
    )
    out_grad = cotangent.astype(jnp.float32)
    moe_grad = lax.all_gather(cotangent, "tensor", axis=0, tiled=True)
    moe_grad_f = moe_grad.astype(jnp.float32)
    gate_part = jnp.einsum("td,tkd->tk", moe_grad_f, part_padded[slot_index], precision=highest)
    gate_grad = lax.psum_scatter(gate_part, "tensor", scatter_dimension=0, tiled=True)
    bias_pick = jnp.einsum("tke,ed->tkd", onehot_own, down_bias, precision=highest)
    gate_grad = gate_grad + jnp.einsum("td,tkd->tk", out_grad, bias_pick, precision=highest)
    prob_grad = jnp.einsum("tk,tke->te", gate_grad, route_own, precision=highest)
    logit_grad = probs_own * (prob_grad - jnp.sum(probs_own * prob_grad, axis=-1, keepdims=True))
    router_grad = jnp.dot(second_low.astype(jnp.float32).T, logit_grad, precision=highest)
    norm_grad_router = jnp.dot(logit_grad, router_full.T, precision=highest)
    slot_values = (gate_vals[:, :, None] * moe_grad_f[:, None, :]).astype(jnp.bfloat16)
    slot_grad = (
        jnp.zeros((spare_slot + 1, model_width), jnp.bfloat16)
        .at[slot_list]
        .set(slot_values.reshape(-1, model_width))[:spare_slot]
        .reshape(experts, CAP, model_width)
    )
    own_values = (
        (gates_own[:, :, None] * out_grad[:, None, :]).astype(jnp.bfloat16).astype(jnp.float32)
    )
    down_bias_grad = jnp.einsum("tke,tkd->ed", route_own, own_values, precision=highest)
    act_grad = jnp.einsum("ecd,efd->ecf", slot_grad, down_used, preferred_element_type=jnp.float32)
    gelu_pull = jax.vjp(lambda entry: jax.nn.gelu(entry, approximate=False), preact)[1]
    preact_grad = gelu_pull(act_grad)[0].astype(jnp.bfloat16)
    down_grad = jnp.einsum("ecf,ecd->efd", activated, slot_grad, preferred_element_type=jnp.float32)
    up_grad = jnp.einsum(
        "ecd,ecf->edf", dispatched, preact_grad, preferred_element_type=jnp.float32
    )
    up_bias_part = jnp.sum(preact_grad.astype(jnp.float32), axis=1)
    expert_summed = (up_grad, down_grad)
    slot_back = jnp.einsum(
        "ecf,edf->ecd", preact_grad, up_used, preferred_element_type=jnp.float32
    ).reshape(spare_slot, model_width)
    back_padded = jnp.concatenate([slot_back, jnp.zeros((1, model_width), jnp.float32)], axis=0)
    picks = slot_index
    norm_grad_second = (
        lax.psum_scatter(
            jnp.sum(back_padded[picks], axis=1).astype(jnp.bfloat16),
            "tensor",
            scatter_dimension=0,
            tiled=True,
        ).astype(jnp.float32)
        + norm_grad_router
    )
    hidden_back, gain_second_grad, shift_second_grad = norm_back(
        norm_grad_second, unit_second, inv_second, gain_second
    )
    hidden_grad = out_grad + hidden_back
    branch_low = hidden_grad.astype(jnp.bfloat16)
    bias_out_grad = jnp.sum(branch_low.astype(jnp.float32), axis=0)
    branch_grad = lax.all_gather(branch_low, "tensor", axis=0, tiled=True)
    mixed_grad = (
        jnp.einsum("td,hd->th", branch_grad, proj_used, preferred_element_type=jnp.float32)
        .astype(jnp.bfloat16)
        .reshape(shape_four)
    )
    proj_grad = jnp.einsum("th,td->hd", mixed_rows, branch_grad, preferred_element_type=jnp.float32)
    scores = (
        jnp.einsum("bqhd,bkhd->bhqk", queries, keys_all, preferred_element_type=jnp.float32)
        * score_scale
    )
    attn_weights = jnp.exp(scores - log_total)
    weight_grad = jnp.einsum(
        "bqhd,bkhd->bhqk", mixed_grad, values_all, preferred_element_type=jnp.float32
    )
    row_dot = jnp.sum(attn_weights * weight_grad, axis=-1, keepdims=True)
    score_grad = (attn_weights * (weight_grad - row_dot)).astype(jnp.bfloat16)
    value_grad = jnp.einsum(
        "bhqk,bqhd->bkhd",
        attn_weights.astype(jnp.bfloat16),
        mixed_grad,
        preferred_element_type=jnp.float32,
    ).astype(jnp.bfloat16)
    query_grad = (
        jnp.einsum("bhqk,bkhd->bqhd", score_grad, keys_all, preferred_element_type=jnp.float32)
        * score_scale
    ).astype(jnp.bfloat16)
    key_grad = (
        jnp.einsum("bhqk,bqhd->bkhd", score_grad, queries, preferred_element_type=jnp.float32)
        * score_scale
    ).astype(jnp.bfloat16)
    triple_grad = jnp.stack(
        [
            query_grad.reshape(group_rows, head_cols),
            key_grad.reshape(group_rows, head_cols),
            value_grad.reshape(group_rows, head_cols),
        ],
        axis=1,
    )
    qkv_grad = jnp.einsum(
        "td,tjh->djh", first_norm, triple_grad, preferred_element_type=jnp.float32
    )
    pair_part = jnp.stack(
        [
            jnp.sum(triple_grad[:, 0].astype(jnp.float32), axis=0),
            jnp.sum(triple_grad[:, 2].astype(jnp.float32), axis=0),
        ],
        axis=0,
    )
    qkv_flat = qkv_used.reshape(model_width, 3 * head_cols)
    piece_rows = triple_grad.reshape(lax.axis_size("tensor") * rows_own, 3 * head_cols)
    first_grad = lax.psum_scatter(
        jnp.einsum("tj,dj->td", piece_rows, qkv_flat, preferred_element_type=jnp.float32).astype(
            jnp.bfloat16
        ),
        "tensor",
        scatter_dimension=0,
        tiled=True,
    ).astype(jnp.float32)
    input_back, gain_first_grad, shift_first_grad = norm_back(
        first_grad, unit_first, inv_first, gain_first
    )
    token_grad = hidden_grad + input_back
    pair_full = lax.dynamic_update_slice_in_dim(
        jnp.zeros((2, model_width), jnp.float32), pair_part, tensor_pos * head_cols, 1
    )
    up_bias_full = lax.dynamic_update_slice_in_dim(
        jnp.zeros((experts, up_bias.shape[1]), jnp.float32), up_bias_part, tensor_pos * ff_cols, 1
    )
    grads_big = (
        lax.psum_scatter(qkv_grad, "dp", scatter_dimension=0, tiled=True),
        lax.psum_scatter(proj_grad, "dp", scatter_dimension=1, tiled=True),
        lax.psum_scatter(expert_summed[0], "dp", scatter_dimension=1, tiled=True),
        lax.psum_scatter(expert_summed[1], "dp", scatter_dimension=2, tiled=True),
    )
    grads_small = (
        lax.psum_scatter(gain_first_grad, ("dp", "tensor"), scatter_dimension=0, tiled=True),
        lax.psum_scatter(shift_first_grad, ("dp", "tensor"), scatter_dimension=0, tiled=True),
        lax.psum_scatter(gain_second_grad, ("dp", "tensor"), scatter_dimension=0, tiled=True),
        lax.psum_scatter(shift_second_grad, ("dp", "tensor"), scatter_dimension=0, tiled=True),
        lax.psum_scatter(pair_full, ("dp", "tensor"), scatter_dimension=1, tiled=True),
        lax.psum_scatter(bias_out_grad, ("dp", "tensor"), scatter_dimension=0, tiled=True),
        lax.psum_scatter(router_grad, ("dp", "tensor"), scatter_dimension=0, tiled=True),
        lax.psum_scatter(up_bias_full, ("dp", "tensor"), scatter_dimension=1, tiled=True),
        lax.psum_scatter(down_bias_grad, ("dp", "tensor"), scatter_dimension=1, tiled=True),
    )
    return (
        final_rows.astype(jnp.bfloat16),
        token_grad,
        grads_small[0],
        grads_small[1],
        grads_big[0],
        grads_small[4],
        grads_big[1],
        grads_small[5],
        grads_small[2],
        grads_small[3],
        grads_small[6],
        grads_big[2],
        grads_small[7],
        grads_big[3],
        grads_small[8],
    )


def solution(mesh):
    return jax.shard_map(
        body,
        mesh=mesh,
        in_specs=(
            P(("dp", "tensor"), None),
            P(("dp", "tensor")),
            P(("dp", "tensor")),
            P("dp", None, "tensor"),
            P(None, ("dp", "tensor")),
            P("tensor", "dp"),
            P(("dp", "tensor")),
            P(("dp", "tensor")),
            P(("dp", "tensor")),
            P(("dp", "tensor"), None),
            P(None, "dp", "tensor"),
            P(None, ("dp", "tensor")),
            P(None, "tensor", "dp"),
            P(None, ("dp", "tensor")),
            P("dp", None),
            P("dp", None),
            P(("dp", "tensor"), None),
        ),
        out_specs=(
            P(("dp", "tensor"), None),
            P(("dp", "tensor"), None),
            P(("dp", "tensor")),
            P(("dp", "tensor")),
            P("dp", None, "tensor"),
            P(None, ("dp", "tensor")),
            P("tensor", "dp"),
            P(("dp", "tensor")),
            P(("dp", "tensor")),
            P(("dp", "tensor")),
            P(("dp", "tensor"), None),
            P(None, "dp", "tensor"),
            P(None, ("dp", "tensor")),
            P(None, "tensor", "dp"),
            P(None, ("dp", "tensor")),
        ),
        check_vma=False,
    )
```

profile of v0, /device:TPU:11, one launch (start us, length us, event | category | flops | bytes accessed | tf_op | source)
XLA Modules:
  0.0 1914.2 jit_solution(14036975859816669289)
XLA Ops:
  11.5 39.7 %all-reduce.26 = (bf16[768]{0:T(1024)(128)(2,1)S(1)}, bf16[768]{0:T(1024)(128)(2,1)S(1)}, bf16[768]{0:T(1024)(128)(2,1)S(1)}, bf16[768]{0:T(1024)(128)(2,1)S(1)}, bf16[768]{0:T(1024)(128)(2,1)S(1)}) all-reduce(bf16[768]{0:T(1024)(128)(2,1)S(1)} %dynamic-update-slice.4, ...), channel_id=1, replica_groups=mesh['dp'=8,'tensor'=4] {'dp','tensor'}, use_global_device_ids=true, to_apply=%add.6 | all-reduce | flops 3840 | bytes 15360
  57.4 25.7 %all_gather.54 = bf16[768,3,192]{2,0,1:T(8,128)(2,1)S(1)} all-gather(bf16[96,3,192]{2,0,1:T(8,128)(2,1)} %param.20), channel_id=1, replica_groups=mesh['dp'=8,'tensor'=4] {'dp'}, dimensions={0}, use_global_device_ids=true | all-gather | bytes 995328 | tf_op jit(solution)/shard_map/all_gather | solution.py:60
  83.8 39.6 %all-gather.1 = bf16[32,24,2]{1,2,0:T(2,128)(2,1)S(1)} all-gather(bf16[1,24,2]{1,2,0:T(2,128)(2,1)S(1)} %bitcast.147), channel_id=1, replica_groups=mesh['dp'=8,'tensor'=4] {'dp','tensor'}, dimensions={0}, use_global_device_ids=true | all-gather | bytes 3168 | tf_op jit(solution)/shard_map/all_gather | solution.py:70
  124.1 28.6 %all_gather.56 = bf16[192,768]{0,1:T(8,128)(2,1)S(1)} all-gather(bf16[192,96]{0,1:T(8,128)(2,1)S(1)} %copy.98), channel_id=1, replica_groups=mesh['dp'=8,'tensor'=4] {'dp'}, dimensions={1}, use_global_device_ids=true | all-gather | bytes 331776 | tf_op jit(solution)/shard_map/all_gather | solution.py:61
  181.8 29.0 %fusion = bf16[400,768]{1,0:T(8,128)(2,1)} fusion(bf16[1576,768]{1,0:T(8,128)(2,1)S(1)} %convolution_convert_fusion), kind=kCustom, calls=%all-reduce-scatter | all-reduce-scatter fusion | flops 1228801 | bytes 3035648
  224.4 35.6 %all-gather.3 = bf16[32,24,8]{1,2,0:T(8,128)(2,1)S(1)} all-gather(bf16[1,24,8]{1,2,0:T(8,128)(2,1)S(1)} %bitcast.144), channel_id=1, replica_groups=mesh['dp'=8,'tensor'=4] {'dp','tensor'}, dimensions={0}, use_global_device_ids=true | all-gather | bytes 12672 | tf_op jit(solution)/shard_map/all_gather | solution.py:72
  261.0 37.0 %all-gather.4 = bf16[32,96,8]{1,2,0:T(8,128)(2,1)S(1)} all-gather(bf16[1,96,8]{1,2,0:T(8,128)(2,1)S(1)} %bitcast.145), channel_id=1, replica_groups=mesh['dp'=8,'tensor'=4] {'dp','tensor'}, dimensions={0}, use_global_device_ids=true | all-gather | bytes 50688 | tf_op jit(solution)/shard_map/all_gather | solution.py:73
  298.9 39.4 %all-gather.5 = bf16[32,24,8]{1,2,0:T(8,128)(2,1)S(1)} all-gather(bf16[1,24,8]{1,2,0:T(8,128)(2,1)S(1)} %bitcast.146), channel_id=1, replica_groups=mesh['dp'=8,'tensor'=4] {'dp','tensor'}, dimensions={0}, use_global_device_ids=true | all-gather | bytes 12672 | tf_op jit(solution)/shard_map/all_gather | solution.py:74
  353.2 22.6 %mul.259 = f32[1576,2,768]{2,1,0:T(2,128)} broadcast(bf16[1576,768]{1,0:T(8,128)(2,1)S(1)} %reshape.245), dimensions={0,2} | broadcast | bytes 12103680 | tf_op jit(solution)/shard_map/mul | solution.py:197
  396.1 34.0 %scatter_custom_fusion.1 = bf16[5041,768]{1,0:T(8,128)(2,1)} fusion(s32[3152]{0:T(1024)S(1)} %fusion.65, f32[3152,768]{1,0:T(8,128)} %mul.260, f32[3152]{0:T(1024)S(1)} %mul.257, bf16[]{:T(256)} %constant.55.clone.1), kind=kCustom, calls=%fused_computation.32 | custom fusion | flops 4841472 | bytes 17442306 | tf_op jit(solution)/shard_map/scatter | solution.py:201
  443.0 22.4 %broadcast_in_dim.12 = bf16[1576,2,768]{2,1,0:T(2,128)(2,1)} broadcast(bf16[1576,768]{1,0:T(8,128)(2,1)S(1)} %reshape.237), dimensions={0,2} | broadcast | bytes 7262208 | tf_op jit(solution)/shard_map/broadcast_in_dim | solution.py:152
  476.3 23.3 %scatter_custom_fusion = bf16[5041,768]{1,0:T(8,128)(2,1)} fusion(s32[3152]{0:T(1024)S(1)} %fusion.65, bf16[3152,768]{1,0:T(8,128)(2,1)} %reshape.206, bf16[]{:T(256)} %constant.55.clone.1), kind=kCustom, calls=%fused_computation.39 | custom fusion | bytes 7743488 | tf_op jit(solution)/shard_map/scatter | solution.py:152
  513.6 18.4 fusion.14
  532.1 49.7 %convert_reduce_fusion = (f32[8,768]{1,0:T(8,128)}, bf16[8,630,768]{2,1,0:T(8,128)(2,1)}, f32[8,630,768]{2,1,0:T(8,128)}) fusion(f32[8,630,768]{2,1,0:T(8,128)} %get-tuple-element.61, f32[8,768]{1,0:T(8,128)S(1)} %dynamic-slice_bitcast_fusion, u8[630,768]{1,0:T(8,128)(4,1)S(1)} %get-tuple-element.16, u8[630,768]{1,0:T(8,128)(4,1)S(1)} %get-tuple-element.15, ...), kind=kOutput, calls=%fused_computation.11 | convolution fusion | flops 6255077376 | bytes 56902656 | tf_op jit(solution)/shard_map/ecd,efd->ecf/dot_general | solution.py:208
  591.0 14.4 fusion.82
  605.5 14.6 reshape.182
  631.9 18.3 gather_fusion
  662.4 36.9 %fusion.84 = f32[1576,1,2]{2,1,0:T(1,128)S(1)} fusion(f32[1576,2,768]{2,1,0:T(2,128)} %reshape.187, bf16[1576,768,1]{1,2,0:T(2,128)(2,1)} %reshape.262), kind=kOutput, calls=%fused_computation.167 | convolution fusion | flops 29048832 | bytes 12116288 | tf_op jit(solution)/shard_map/td,tkd->tk/dot_general | solution.py:189
  714.2 14.8 fusion.83
  755.3 18.3 gather_fusion.1
  785.8 44.4 %reduce_sum.225 = bf16[1576,768]{1,0:T(8,128)(2,1)} reduce(f32[1576,2,768]{2,1,0:T(2,128)} %reshape.199, f32[]{:T(128)} %constant.46.clone.1), dimensions={1}, to_apply=%region_15.16 | reduce | flops 1210368 | bytes 12103684 | tf_op jit(solution)/shard_map/reduce_sum | solution.py:224
  830.3 24.4 %fusion.2 = bf16[400,768]{1,0:T(8,128)(2,1)S(1)} fusion(bf16[1576,768]{1,0:T(8,128)(2,1)} %reduce_sum.225), kind=kCustom, calls=%all-reduce-scatter.2 | all-reduce-scatter fusion | flops 1228801 | bytes 3035648
  870.3 15.6 multiply_reduce_fusion
  887.0 14.8 all-gather.25.cloned.1.call-done
  946.5 48.5 %fusion.78 = (bf16[400,768]{1,0:T(8,128)(2,1)}, bf16[400,768]{1,0:T(8,128)(2,1)S(1)}) fusion(bf16[1576,768]{1,0:T(8,128)(2,1)} %multiply_reduce_fusion, bf16[1576,768]{1,0:T(8,128)(2,1)} %bitcast_convert_fusion), kind=kCustom, calls=%all-reduce-scatter.5 | all-reduce-scatter fusion | flops 2457601 | bytes 6070784
  1013.4 16.3 fusion.87
  1029.8 16.2 fusion.86
  1061.8 72.3 %all-reduce.30.cloned.1.call-done = (f32[768]{0:T(1024)}, f32[768]{0:T(1024)}, f32[2,768]{1,0:T(2,128)}, f32[768]{0:T(1024)}, f32[768]{0:T(1024)}, /*index=5*/f3...) async-done(((f32[768]{0:T(1024)}, f32[768]{0:T(1024)}, f32[2,768]{1,0:T(2,128)}, f32[768]{0:T(1024)}, f32[768]{0:T(1024)}, /*index=5*/f32[768]{0:T(1024)}, f32[768,8]{0,1:T(8,128)}, ...) | async-done | bytes 70672
  1144.4 56.9 %reduce-scatter.29.cloned.1.call-done = f32[96,192]{1,0:T(8,128)} async-done(((f32[768,192]{1,0:T(8,128)}), f32[96,192]{1,0:T(8,128)}) %reduce-scatter.29.cloned.1.call-update) | async-done | bytes 73744
  1202.9 69.6 %reduce-scatter.23.cloned.1.call-done = f32[96,3,192]{2,0,1:T(8,128)} async-done(((f32[768,3,192]{2,0,1:T(8,128)}), f32[96,3,192]{2,0,1:T(8,128)}) %reduce-scatter.23.cloned.1.call-update) | async-done | bytes 221200 | tf_op jit(solution)/shard_map/reduce_scatter | solution.py:307
  1272.5 318.0 %reduce-scatter.27.cloned.1.call-done = f32[8,768,96]{1,2,0:T(8,128)} async-done(((f32[8,768,768]{1,2,0:T(8,128)}), f32[8,768,96]{1,2,0:T(8,128)}) %reduce-scatter.27.cloned.1.call-update) | async-done | bytes 2359312 | tf_op jit(solution)/shard_map/reduce_scatter | solution.py:310
  1590.5 316.3 %reduce-scatter.25.cloned.1.call-done = f32[8,96,768]{2,1,0:T(8,128)} async-done(((f32[8,768,768]{2,1,0:T(8,128)}), f32[8,96,768]{2,1,0:T(8,128)}) %reduce-scatter.25.cloned.1.call-update) | async-done | bytes 2359312 | tf_op jit(solution)/shard_map/reduce_scatter | solution.py:309
  (339 shorter events, 321.8 us)
Async XLA Ops:
  7.2 76.6 %copy-start.67 = (bf16[2,24]{1,0:T(2,128)(2,1)S(1)}, bf16[2,24]{1,0:T(2,128)(2,1)}, u32[]{:S(2)}) copy-start(bf16[2,24]{1,0:T(2,128)(2,1)} %param.21) | copy-start | bytes 292
  7.2 116.8 %copy-start.47 = (bf16[192,96]{1,0:T(8,128)(2,1)S(1)}, bf16[192,96]{1,0:T(8,128)(2,1)}, u32[]{:S(2)}) copy-start(bf16[192,96]{1,0:T(8,128)(2,1)} %param.22) | copy-start | bytes 110596
  7.2 145.5 %all-gather.19.cloned.1.call-start = ((), (), s32[]{:S(2)}) async-start(), calls=%async_computation.10 | async-start | bytes 3072000 | tf_op jit(solution)/shard_map/all_gather | solution.py:98
  56.6 294.3 %all-gather.23.cloned.1.call-start = ((), (), s32[]{:S(2)}) async-start(), calls=%async_computation.12 | async-start | bytes 3072000 | tf_op jit(solution)/shard_map/all_gather | solution.py:187
  57.3 334.3 %all-gather.21.cloned.1.call-start = ((), (), s32[]{:S(2)}) async-start(), calls=%async_computation.11 | async-start | bytes 3072000 | tf_op jit(solution)/shard_map/all_gather | solution.py:138
  83.1 77.0 %copy-start.22 = (bf16[768,3,192]{2,0,1:T(8,128)(2,1)}, bf16[768,3,192]{2,0,1:T(8,128)(2,1)S(1)}, u32[]{:S(2)}) copy-start(bf16[768,3,192]{2,0,1:T(8,128)(2,1)S(1)} %all_gather.54) | copy-start | bytes 2654212
  211.6 6.2 collective-permute-start
  220.8 77.3 %copy-start.4 = (bf16[418,768]{1,0:T(8,128)(2,1)}, bf16[418,768]{1,0:T(8,128)(2,1)S(1)}, u32[]{:S(2)}) copy-start(bf16[418,768]{1,0:T(8,128)(2,1)S(1)} %concatenate.8) | copy-start | bytes 1926148
  221.2 77.6 %copy-start.66 = (bf16[8,24]{1,0:T(8,128)(2,1)S(1)}, bf16[8,24]{1,0:T(8,128)(2,1)}, u32[]{:S(2)}) copy-start(bf16[8,24]{1,0:T(8,128)(2,1)} %param.30) | copy-start | bytes 1156
  223.1 117.4 %copy-start.20 = (bf16[394,768]{1,0:T(8,128)(2,1)S(1)}, bf16[394,768]{1,0:T(8,128)(2,1)}, u32[]{:S(2)}) copy-start(bf16[394,768]{1,0:T(8,128)(2,1)} %param.33) | copy-start | bytes 1815556
  223.1 290.4 %all-gather.15.cloned.1.call-start = ((), (), s32[]{:S(2)}) async-start(), calls=%async_computation.5 | async-start | bytes 10616832 | tf_op jit(solution)/shard_map/all_gather | solution.py:62
  223.7 308.3 %all-gather.17.cloned.1.call-start = ((), (), s32[]{:S(2)}) async-start(), calls=%async_computation.6 | async-start | bytes 10616832 | tf_op jit(solution)/shard_map/all_gather | solution.py:63
  224.3 677.5 %all-gather.25.cloned.1.call-start = ((), (), s32[]{:S(2)}) async-start(), calls=%async_computation.13 | async-start | bytes 3072000 | tf_op jit(solution)/shard_map/all_gather | solution.py:237
  260.2 133.8 %copy-start.45 = (bf16[768,8]{0,1:T(8,128)(2,1)}, bf16[768,8]{0,1:T(8,128)(2,1)S(1)}, u32[]{:S(2)}) copy-start(bf16[768,8]{0,1:T(8,128)(2,1)S(1)} %reshape.239) | copy-start | bytes 36868
  709.9 149.2 %collective-permute-start.3 = (f32[18,2]{1,0:T(8,128)S(1)}, f32[18,2]{1,0:T(8,128)S(1)}, u32[]{:S(2)}, u32[]{:S(2)}) collective-permute-start(f32[18,2]{1,0:T(8,128)S(1)} %slice.43), channel_id=1, source_target_pairs={{0,1},{1,2},{2,3},{4,5},{5,6},{6,7},{8,9},{9,10},{10,11},{12,13},{... | collective-permute-start | bytes 440
  785.8 73.9 %copy-start.34 = (f32[394,1,2]{2,1,0:T(1,128)S(1)}, f32[394,1,2]{2,1,0:T(1,128)}, u32[]{:S(2)}) copy-start(f32[394,1,2]{2,1,0:T(1,128)} %fusion.19) | copy-start | bytes 9460
  785.8 74.0 %copy-start.40 = (pred[1576,2,8]{0,2,1:T(8,128)(4,1)S(1)}, pred[1576,2,8]{0,2,1:T(8,128)(4,1)}, u32[]{:S(2)}) copy-start(pred[1576,2,8]{0,2,1:T(8,128)(4,1)} %copy-done.39) | copy-start | bytes 75652
  785.8 74.0 %copy-start.48 = (f32[394,2]{0,1:T(2,128)S(1)}, f32[394,2]{0,1:T(2,128)}, u32[]{:S(2)}) copy-start(f32[394,2]{0,1:T(2,128)} %constant_dynamic-slice_fusion) | copy-start | bytes 9460
  785.8 74.0 %copy-start.49 = (f32[394,2]{0,1:T(2,128)S(1)}, f32[394,2]{0,1:T(2,128)}, u32[]{:S(2)}) copy-start(f32[394,2]{0,1:T(2,128)} %dynamic-slice_convert_fusion) | copy-start | bytes 9460
  785.8 74.1 %copy-start.32 = (f32[1576,8]{0,1:T(8,128)S(1)}, f32[1576,8]{0,1:T(8,128)}, u32[]{:S(2)}) copy-start(f32[1576,8]{0,1:T(8,128)} %copy-done.31) | copy-start | bytes 151300
  854.7 5.4 collective-permute-start.2
  867.1 184.4 %reduce-scatter.31.cloned.1.call-start = ((), (), s32[]{:S(2)}) async-start(), calls=%async_computation.15 | async-start | bytes 1622016
  886.0 248.1 %all-reduce.30.cloned.1.call-start = ((), (), s32[]{:S(2)}) async-start(), calls=%async_computation.16 | async-start | bytes 151552
  946.5 55.4 %copy-start.42 = (f32[768]{0:T(1024)S(1)}, f32[768]{0:T(1024)}, u32[]{:S(2)}) copy-start(f32[768]{0:T(1024)} %copy-done.41) | copy-start | bytes 9220
  946.5 55.4 %copy-start.44 = (f32[394]{0:T(512)S(1)}, f32[394]{0:T(512)}, u32[]{:S(2)}) copy-start(f32[394]{0:T(512)} %copy-done.43) | copy-start | bytes 4732
  946.5 55.4 %copy-start.53 = (f32[394]{0:T(512)S(1)}, f32[394]{0:T(512)}, u32[]{:S(2)}) copy-start(f32[394]{0:T(512)} %copy-done.52) | copy-start | bytes 4732
  995.0 5.4 collective-permute-start.4
  1003.3 198.0 %reduce-scatter.29.cloned.1.call-start = ((), (), s32[]{:S(2)}) async-start(), calls=%async_computation.14 | async-start | bytes 884736
  1007.3 265.2 %reduce-scatter.23.cloned.1.call-start = ((), (), s32[]{:S(2)}) async-start(), calls=%async_computation.7 | async-start | bytes 2654208 | tf_op jit(solution)/shard_map/reduce_scatter | solution.py:307
  1013.4 577.1 %reduce-scatter.27.cloned.1.call-start = ((), (), s32[]{:S(2)}) async-start(), calls=%async_computation.9 | async-start | bytes 21233664 | tf_op jit(solution)/shard_map/reduce_scatter | solution.py:310
  1029.8 877.0 %reduce-scatter.25.cloned.1.call-start = ((), (), s32[]{:S(2)}) async-start(), calls=%async_computation.8 | async-start | bytes 21233664 | tf_op jit(solution)/shard_map/reduce_scatter | solution.py:309
  1047.0 5.9 collective-permute-start.1
  (56 other events, 947.5 us)
Sparse Core Ops, SparseCore 0:
  56.7 25.7 all-gather.18
  84.1 24.7 all-gather.22
  223.3 29.2 all-gather.20
  254.6 135.0 all-gather.14
  391.8 136.1 all-gather.16
  867.2 34.5 all-gather.24
  907.1 97.8 reduce-scatter.30
  1011.9 122.1 all-reduce.29
  1137.7 63.4 reduce-scatter.28
  1205.2 67.2 reduce-scatter.22
  1277.0 313.4 reduce-scatter.26
  1594.8 311.9 reduce-scatter.24
where the time goes:
time: 1920 us; the launch traced here: 1910 us
  waiting for transfers between devices  851 us (44%)
  blocking collectives  358 us (19%)
  local copies, waits for them, and re-layouts  321 us (17%)
  matrix products  227 us (12%)
  other arithmetic  118 us (6%)
  starting transfers between devices  22.8 us (1%)
    reduce_scatter x1, waiting for transfers between devices, body(): lax.psum_scatter(expert_summed[1], 'dp', scatter_dimension=2, tiled=True)  318 us
    reduce_scatter x1, waiting for transfers between devices, body(): lax.psum_scatter(expert_summed[0], 'dp', scatter_dimension=1, tiled=True)  316 us
    unnamed x5, blocking collectives  152 us
    unnamed x20, waiting for transfers between devices  132 us
    reduce_scatter x1, waiting for transfers between devices, body(): lax.psum_scatter(qkv_grad, 'dp', scatter_dimension=0, tiled=True)  69.6 us
    unnamed x186, local copies, waits for them, and re-layouts  56.7 us
    dot_general x1, matrix products, body(): jnp.einsum('ecd,efd->ecf', slot_grad, down_used, preferred_element_type=j...  49.7 us
    reduce_sum x1, other arithmetic, body(): jnp.sum(back_padded[picks], axis=1).astype(jnp.bfloat16)  44.4 us
  transfers between devices with their start and end apart: 17, of which 8 were waited for; matrix products, arithmetic and copies ran while one was open for 30% of the time, Pallas kernels for 0%

commit v1 on v0

v1 whole, which is shorter than its diff:
```python
import functools

import jax
import jax.numpy as jnp
from jax import lax
from jax.experimental import pallas as pl
from jax.experimental.pallas import tpu as pltpu
from jax.sharding import PartitionSpec as P

HEAD_DIM = 64
SEQ = 197
SEQ_PAD = 208
CAP = 630
CAP_PAD = 640
EPS = 1e-6
BF = jnp.bfloat16
F32 = jnp.float32
MESH = pl.DeviceIdType.MESH
VMEM_LIMIT = 56 * 1024 * 1024
VM = pl.BlockSpec(memory_space=pltpu.VMEM)
HB = pl.BlockSpec(memory_space=pl.ANY)


def nn(a, b):
    return lax.dot_general(a, b, (((1,), (0,)), ((), ())), preferred_element_type=F32)


def nt(a, b):
    return lax.dot_general(a, b, (((1,), (1,)), ((), ())), preferred_element_type=F32)


def tn(a, b):
    return lax.dot_general(a, b, (((0,), (0,)), ((), ())), preferred_element_type=F32)


def unit_norm(rows):
    centred = rows - jnp.mean(rows, axis=-1, keepdims=True)
    inv = lax.rsqrt(jnp.mean(centred * centred, axis=-1, keepdims=True) + EPS)
    return centred * inv, inv


def place(cells):
    index = lax.axis_index("dp")
    return lax.div(index, cells), lax.rem(index, cells), lax.axis_index("tensor")


def tensor_peers(t):
    core = t + 1 - 2 * lax.rem(t, 2)
    side = lax.rem(t + 2, 4)
    return core, side, lax.rem(core + 2, 4)


def remote(src, dst, send, recv, device):
    return pltpu.make_async_remote_copy(
        src_ref=src, dst_ref=dst, send_sem=send, recv_sem=recv, device_id=device, device_id_type=MESH
    )


def signal(barrier, device):
    pl.semaphore_signal(barrier, inc=1, device_id=device, device_id_type=MESH)


def gather_kernel(cells, n_shared, *refs):
    n_arr = n_shared + 1
    srcs, cot = refs[:n_arr], refs[n_arr]
    dsts, cot_all = refs[n_arr + 1 : 2 * n_arr + 1], refs[2 * n_arr + 1]
    (dp_s, dp_r, y_s, y_r, c_s, c_r, f_s, f_r, own, cot_s, cot_r) = refs[2 * n_arr + 2 :]
    d, cell, t = place(cells)
    core, side, far = tensor_peers(t)
    here = d * cells + cell

    def at_dp(k):
        return (lax.rem(d + k, 8) * cells + cell, t)

    barrier = pltpu.get_barrier_semaphore()
    for k in range(1, 8):
        signal(barrier, at_dp(k))
    signal(barrier, (here, core))
    signal(barrier, (here, side))
    pl.semaphore_wait(barrier, 9)

    waits = []
    locals_ = []
    for a in range(n_arr):
        shared = a < n_shared
        mine = pltpu.make_async_copy(srcs[a] if shared else srcs[a].at[d], dsts[a].at[t, d], own.at[a])
        mine.start()
        locals_.append(mine)
    dp_copies = []
    for a in range(n_arr):
        shared = a < n_shared
        row = []
        for k in range(1, 8):
            p = lax.rem(d + k, 8)
            copy = remote(
                srcs[a] if shared else srcs[a].at[p],
                dsts[a].at[t, d],
                dp_s.at[a, k],
                dp_r.at[a, k],
                at_dp(k),
            )
            copy.start()
            row.append(copy)
        dp_copies.append(row)
    cot_y = remote(cot, cot_all.at[t], cot_s.at[0], cot_r.at[0], (here, side))
    cot_c = remote(cot, cot_all.at[t], cot_s.at[1], cot_r.at[1], (here, core))
    cot_own = pltpu.make_async_copy(cot, cot_all.at[t], own.at[n_arr])
    cot_y.start()
    cot_c.start()
    cot_own.start()

    side_copies = [[None] * 8 for _ in range(n_arr)]

    def spread(a):
        for k in range(8):
            s = lax.rem(d + 8 - k, 8)
            block = dsts[a].at[t, s]
            if k == 0:
                locals_[a].wait()
            else:
                dp_copies[a][k - 1].wait_recv()
            over = remote(block, block, y_s.at[a, k], y_r.at[a, k], (here, side))
            over.start()
            side_copies[a][k] = over
            near = remote(block, block, c_s.at[a, k], c_r.at[a, k], (here, core))
            near.start()
            waits.append(near)

    def forward(a):
        for k in range(8):
            s = lax.rem(d + 8 - k, 8)
            block = dsts[a].at[side, s]
            side_copies[a][k].wait_recv()
            near = remote(block, block, f_s.at[a, k], f_r.at[a, k], (here, core))
            near.start()
            waits.append(near)

    for a in range(n_arr):
        spread(a)
        if a:
            forward(a - 1)
        if a == n_arr - 1:
            cot_y.wait_recv()
            cot_f = remote(cot_all.at[side], cot_all.at[side], cot_s.at[2], cot_r.at[2], (here, core))
            cot_f.start()
    forward(n_arr - 1)
    for copy in waits:
        copy.wait()
    for a in range(n_arr):
        for copy in dp_copies[a]:
            copy.wait_send()
        for copy in side_copies[a]:
            copy.wait_send()
    cot_y.wait_send()
    cot_c.wait()
    cot_f.wait()
    cot_own.wait()


def gather_weights(cells, shared, expert, cot):
    arrays = list(shared) + [expert]
    n_arr = len(arrays)
    shapes = [jax.ShapeDtypeStruct((4, 8) + a.shape, a.dtype) for a in shared]
    shapes.append(jax.ShapeDtypeStruct((4,) + expert.shape, expert.dtype))
    shapes.append(jax.ShapeDtypeStruct((4,) + cot.shape, cot.dtype))
    dma = pltpu.SemaphoreType.DMA
    return pl.pallas_call(
        functools.partial(gather_kernel, cells, len(shared)),
        out_shape=shapes,
        in_specs=[HB] * (n_arr + 1),
        out_specs=[HB] * (n_arr + 1),
        scratch_shapes=[dma((n_arr, 8))] * 8 + [dma((n_arr + 1,)), dma((3,)), dma((3,))],
        compiler_params=pltpu.CompilerParams(collective_id=0, has_side_effects=True),
        name="gather_weights",
    )(*arrays, cot)


def softmax_rows(q, k):
    scores = nt(q, k) * (HEAD_DIM**-0.5)
    lane = lax.broadcasted_iota(jnp.int32, scores.shape, 1)
    scores = jnp.where(lane < SEQ, scores, -1e30)
    raised = jnp.exp(scores - jnp.max(scores, axis=-1, keepdims=True))
    return raised / jnp.sum(raised, axis=-1, keepdims=True)


def attention_kernel(tok, vec, qkv_bias, router, wall, second_out, hidden_out, probs_out, qkv_out, mixed_out, acc):
    rows = tok.shape[0]
    heads = qkv_out.shape[2] // 3
    inputs = tok[...].astype(F32)
    unit, _ = unit_norm(inputs)
    first = (unit * vec[0:1] + vec[1:2]).astype(BF)
    acc[...] = inputs + vec[4:5]

    def step(t, carry):
        weights = wall[t]
        qkv = (nn(first, weights[:, : 3 * heads]) + qkv_bias[t][0:1]).astype(BF)
        qkv_out[t] = qkv
        mixed = []
        for i in range(rows // SEQ_PAD):
            part = qkv[i * SEQ_PAD : (i + 1) * SEQ_PAD]
            sides = []
            for h in range(heads // HEAD_DIM):
                q, k, v = (part[:, j * heads + h * HEAD_DIM : j * heads + (h + 1) * HEAD_DIM] for j in range(3))
                sides.append(nn(softmax_rows(q, k).astype(BF), v).astype(BF))
            mixed.append(jnp.concatenate(sides, axis=1))
        mixed = jnp.concatenate(mixed, axis=0)
        mixed_out[t] = mixed
        acc[...] += nt(mixed, weights[:, 3 * heads :])
        return carry

    lax.fori_loop(0, 4, step, 0)
    hidden = acc[...]
    hidden_out[...] = hidden
    unit, _ = unit_norm(hidden)
    second = (unit * vec[2:3] + vec[3:4]).astype(BF)
    second_out[...] = second
    logits = nt(router[...], second)
    raised = jnp.exp(logits - jnp.max(logits, axis=0, keepdims=True))
    probs_out[...] = raised / jnp.sum(raised, axis=0, keepdims=True)


def dispatch_kernel(
    cells, second, probs, slots, cot_all, x_out, g_out, probs_all, sec_all, x_buf, g_buf, raw,
    ag_s, ag_r, x_s, x_r, own,
):
    d, cell, t = place(cells)
    core, side, far = tensor_peers(t)
    here = d * cells + cell
    line = lax.rem(d, 4)
    mine = lax.div(d, 4)
    loop = line == t

    def partner(j):
        return ((t + 4 * j) * cells + cell, line)

    def is_self(j):
        return jnp.logical_and(loop, mine == j)

    barrier = pltpu.get_barrier_semaphore()
    signal(barrier, (here, core))
    signal(barrier, (here, side))
    for j in range(2):

        @pl.when(jnp.logical_not(is_self(j)))
        def _():
            signal(barrier, partner(j))

    pl.semaphore_wait(barrier, jnp.where(loop, 3, 4))

    pairs = []
    for n, (src, dst) in enumerate(((second, sec_all), (probs, probs_all))):
        over = remote(src, dst.at[t], ag_s.at[n, 0], ag_r.at[n, 0], (here, side))
        near = remote(src, dst.at[t], ag_s.at[n, 1], ag_r.at[n, 1], (here, core))
        over.start()
        near.start()
        pairs.append((over, near))
    sec_all[t] = second[...]
    probs_all[t] = probs[...]

    def onehot(tt, e):
        slot = slots[tt, pl.ds(e, 1), :]
        return lax.broadcasted_iota(jnp.int32, (CAP_PAD, slot.shape[1]), 0) == slot

    def pick(e, rows):
        total = None
        for tt in range(4):
            part = nn(onehot(tt, e).astype(F32).astype(BF), rows[tt])
            total = part if total is None else total + part
        return total

    for j in range(2):
        raw[j] = pick(t + 4 * j, cot_all).astype(BF)

    forwards = []
    for n, dst in enumerate((sec_all, probs_all)):
        pairs[n][0].wait_recv()
        along = remote(dst.at[side], dst.at[side], ag_s.at[n, 2], ag_r.at[n, 2], (here, core))
        along.start()
        forwards.append(along)
    for n in range(2):
        pairs[n][1].wait_recv()
        forwards[n].wait_recv()

    def send(j, n, buf, out):
        copy = remote(buf.at[j], out.at[mine], x_s.at[n, j], x_r.at[n, mine], partner(j))

        @pl.when(is_self(j))
        def _():
            pltpu.make_async_copy(buf.at[j], out.at[mine], own.at[n]).start()

        @pl.when(jnp.logical_not(is_self(j)))
        def _():
            copy.start()

        return copy

    sent = []
    for j in range(2):
        x_buf[j] = pick(t + 4 * j, sec_all).astype(BF)
        sent.append((j, 0, x_buf, x_out, send(j, 0, x_buf, x_out)))
    for j in range(2):
        e = t + 4 * j
        gate = None
        for tt in range(4):
            part = jnp.sum(
                jnp.where(onehot(tt, e), probs_all[tt, pl.ds(e, 1), :], 0.0), axis=1, keepdims=True
            )
            gate = part if gate is None else gate + part
        g_buf[j] = (gate * raw[j].astype(F32)).astype(BF)
        sent.append((j, 1, g_buf, g_out, send(j, 1, g_buf, g_out)))

    for j, n, buf, out, copy in sent:

        @pl.when(is_self(j))
        def _():
            pltpu.make_async_copy(buf.at[j], out.at[mine], own.at[n]).wait()

        @pl.when(jnp.logical_not(is_self(j)))
        def _():
            copy.wait_send()
            remote(buf.at[j], out.at[j], x_s.at[n, j], x_r.at[n, j], partner(j)).wait_recv()

    for n in range(2):
        for copy in pairs[n]:
            copy.wait_send()
        forwards[n].wait_send()


def gelu_both(x):
    phi = 0.5 * (1.0 + lax.erf(x * (0.5**0.5)))
    slope = phi + x * (jnp.exp(-0.5 * x * x) * 0.3989422804014327)
    return x * phi, slope


def expert_kernel(
    x_ref, g_ref, w_ref, up_bias, down_bias, y_out, b_out, q_out, dw_out, dup_out, ddown_out,
    y_acc, b_acc, x_turned, g_turned, act_buf, pre_buf,
):
    step = pl.program_id(0)
    slots, width = y_acc.shape
    tile = 256
    w_in = w_ref[0, :, 0].reshape(width, -1)
    w_out = w_ref[0, :, 1].reshape(width, -1)

    @pl.when(step == 0)
    def _():
        y_acc[...] = jnp.broadcast_to(down_bias[...], y_acc.shape)
        b_acc[...] = jnp.zeros_like(b_acc)
        x_turned[...] = x_ref[...].T
        g_turned[...] = g_ref[...].T
        ddown_out[...] = jnp.sum(g_ref[...].astype(F32), axis=0, keepdims=True)

    def rows_step(m, bias_sum):
        here = pl.ds(pl.multiple_of(m * tile, tile), tile)
        x, g = x_ref[here, :], g_ref[here, :]
        pre = nn(x, w_in) + up_bias[0]
        act, slope = gelu_both(pre)
        act = act.astype(BF)
        act_buf[here, :] = act
        pre_grad = (nn(g, w_out) * slope).astype(BF)
        pre_buf[here, :] = pre_grad
        y_acc[here, :] += nt(act, w_out)
        b_acc[here, :] += nt(pre_grad, w_in)
        return bias_sum + jnp.sum(pre_grad.astype(F32), axis=0, keepdims=True)

    ff = w_in.shape[1]
    dup_out[0] = lax.fori_loop(0, slots // tile, rows_step, jnp.zeros((1, ff), F32))

    def grad_step(n, carry):
        here = pl.ds(pl.multiple_of(n * 192, 192), 192)
        d_in = nn(x_turned[here, :], pre_buf[...]).astype(BF)
        d_out = nn(g_turned[here, :], act_buf[...]).astype(BF)
        pair = pl.ds(2 * n, 2)
        dw_out[0, pair, 0] = d_in.reshape(2, 96, ff)
        dw_out[0, pair, 1] = d_out.reshape(2, 96, ff)
        return carry

    lax.fori_loop(0, width // 192, grad_step, 0)

    @pl.when(step == pl.num_programs(0) - 1)
    def _():
        ones = jnp.ones((8, width), BF)
        for m in range(slots // 128):
            here = slice(m * 128, (m + 1) * 128)
            y = y_acc[here, :]
            y_out[here, :] = y.astype(BF)
            b_out[here, :] = b_acc[here, :].astype(BF)
            z = y * g_ref[here, :].astype(F32)
            high = z.astype(BF)
            low = (z - high.astype(F32)).astype(BF)
            half, place_ = divmod(m * 128, slots // 2)
            q_out[half, :, place_ : place_ + 128] = nt(ones, high) + nt(ones, low)


def combine_kernel(
    cells, b_src, y_src, q_src, slots, probs, r_out, m_out, q_all, b_in, y_in, blocks, core_in, side_buf, side_in,
    a_s, a_r, q_s, q_r, c_s, c_r, y_s, y_r, own,
):
    d, cell, t = place(cells)
    core, side, far = tensor_peers(t)
    here = d * cells + cell
    line = lax.rem(d, 4)
    mine = lax.div(d, 4)
    loop = line == t

    def partner(j):
        return ((t + 4 * j) * cells + cell, line)

    def is_self(j):
        return jnp.logical_and(loop, mine == j)

    barrier = pltpu.get_barrier_semaphore()
    signal(barrier, (here, core))
    signal(barrier, (here, side))
    for e in range(8):

        @pl.when(jnp.logical_not(jnp.logical_and(loop, d == e)))
        def _():
            signal(barrier, (e * cells + cell, line))

    pl.semaphore_wait(barrier, jnp.where(loop, 9, 10))

    for n, (src, dst) in enumerate(((b_src, b_in), (y_src, y_in))):
        for j in range(2):

            @pl.when(is_self(j))
            def _():
                pltpu.make_async_copy(src.at[j], dst.at[mine], own.at[n]).start()

            @pl.when(jnp.logical_not(is_self(j)))
            def _():
                remote(src.at[j], dst.at[mine], a_s.at[n, j], a_r.at[n, mine], partner(j)).start()

        if n == 0:
            for j in range(2):
                for tt in range(4):
                    itself = jnp.logical_and(t + 4 * j == d, t == tt)

                    @pl.when(itself)
                    def _():
                        pltpu.make_async_copy(q_src.at[j], q_all.at[d], own.at[2]).start()

                    @pl.when(jnp.logical_not(itself))
                    def _():
                        remote(
                            q_src.at[j], q_all.at[d], q_s.at[j, tt], q_r.at[d], ((t + 4 * j) * cells + cell, tt)
                        ).start()

    for n, (src, dst) in enumerate(((b_src, b_in), (y_src, y_in))):
        for j in range(2):

            @pl.when(is_self(j))
            def _():
                pltpu.make_async_copy(src.at[j], dst.at[mine], own.at[n]).wait()

            @pl.when(jnp.logical_not(is_self(j)))
            def _():
                remote(src.at[j], dst.at[j], a_s.at[n, j], a_r.at[n, j], partner(j)).wait_recv()

    def block(tt):
        total_b = total_y = None
        table, gates = slots[tt], probs[tt]
        lane = lax.broadcasted_iota(jnp.int32, table.shape, 1)
        for j in range(2):
            e = t + 4 * j
            slot = jnp.sum(jnp.where(lane == e, table, 0.0), axis=1, keepdims=True)
            gate = jnp.sum(jnp.where(lane == e, gates, 0.0), axis=1, keepdims=True)
            at = lax.broadcasted_iota(jnp.int32, (table.shape[0], CAP_PAD), 1)
            hot = (at == slot.astype(jnp.int32)).astype(F32).astype(BF)
            part_b = nn(hot, b_in[j])
            part_y = nn(hot, y_in[j]) * gate
            total_b = part_b if j == 0 else total_b + part_b
            total_y = part_y if j == 0 else total_y + part_y
        return total_b, total_y

    core_copies = []
    for i, tt in enumerate((far, core)):
        total_b, total_y = block(tt)
        blocks[i, 0] = total_b.astype(BF)
        blocks[i, 1] = total_y.astype(BF)
        copy = remote(blocks.at[i], core_in.at[i], c_s.at[i], c_r.at[i], (here, core))
        copy.start()
        core_copies.append(copy)
    total_b, total_y = block(side)
    core_copies[0].wait_recv()
    side_buf[0] = (total_b + core_in[0, 0].astype(F32)).astype(BF)
    side_buf[1] = (total_y + core_in[0, 1].astype(F32)).astype(BF)
    side_copy = remote(side_buf, side_in, y_s.at[0], y_r.at[0], (here, side))
    side_copy.start()
    total_b, total_y = block(t)
    core_copies[1].wait_recv()
    total_b = total_b + core_in[1, 0].astype(F32)
    total_y = total_y + core_in[1, 1].astype(F32)
    side_copy.wait_recv()
    r_out[...] = total_b + side_in[0].astype(F32)
    m_out[...] = total_y + side_in[1].astype(F32)

    for copy in core_copies:
        copy.wait_send()
    side_copy.wait_send()
    for n, (src, dst) in enumerate(((b_src, b_in), (y_src, y_in))):
        for j in range(2):

            @pl.when(jnp.logical_not(is_self(j)))
            def _():
                remote(src.at[j], dst.at[mine], a_s.at[n, j], a_r.at[n, mine], partner(j)).wait_send()

    for j in range(2):
        for tt in range(4):
            itself = jnp.logical_and(t + 4 * j == d, t == tt)

            @pl.when(itself)
            def _():
                pltpu.make_async_copy(q_src.at[j], q_all.at[d], own.at[2]).wait()

            @pl.when(jnp.logical_not(itself))
            def _():
                remote(
                    q_src.at[j], q_all.at[d], q_s.at[j, tt], q_r.at[d], ((t + 4 * j) * cells + cell, tt)
                ).wait_send()

    for e in range(8):

        @pl.when(jnp.logical_not(jnp.logical_and(loop, d == e)))
        def _():
            remote(q_src.at[0], q_all.at[e], q_s.at[0, 0], q_r.at[e], (e * cells + cell, line)).wait_recv()


def backward_kernel(
    tok, hid, r_ref, m_ref, cot, probs, q_all, slots, router, vec, wall, qkv_ref, mixed_ref,
    out, token_grad, dw_out, vec_out, bias_out, n1,
):
    heads = qkv_ref.shape[2] // 3
    rows = tok.shape[0]
    hidden = hid[...]
    out[...] = (hidden + m_ref[...]).astype(BF)
    picked = jnp.zeros(probs.shape, F32)
    sub = lax.broadcasted_iota(jnp.int32, probs.shape, 0)
    for e in range(8):
        hot = (lax.broadcasted_iota(jnp.int32, (CAP_PAD, rows), 0) == slots[e : e + 1, :]).astype(F32).astype(BF)
        q = q_all[e]
        high = q.astype(BF)
        low = (q - high.astype(F32)).astype(BF)
        picked = jnp.where(sub == e, nn(high, hot) + nn(low, hot), picked)
    logit = picked - probs[...] * jnp.sum(picked, axis=0, keepdims=True)
    high = logit.astype(BF)
    both = jnp.concatenate([high, (logit - high.astype(F32)).astype(BF)], axis=0)
    unit, inv = unit_norm(hidden)
    gain = vec[2:3]
    second = (unit * gain + vec[3:4]).astype(BF)
    router_grad = nn(both, second)
    vec_out[8:16] = router_grad[0:8] + router_grad[8:16]
    table = router[...]
    n2 = r_ref[...] + tn(both, jnp.concatenate([table, table], axis=0))
    vec_out[2:3] = jnp.sum(n2 * unit, axis=0, keepdims=True)
    vec_out[3:4] = jnp.sum(n2, axis=0, keepdims=True)
    scaled = n2 * gain
    back = inv * (
        scaled
        - jnp.mean(scaled, axis=-1, keepdims=True)
        - unit * jnp.mean(scaled * unit, axis=-1, keepdims=True)
    )
    hidden_grad = cot[...].astype(F32) + back
    token_grad[...] = hidden_grad
    branch = hidden_grad.astype(BF)
    vec_out[4:5] = jnp.sum(branch.astype(F32), axis=0, keepdims=True)
    vec_out[5:8] = jnp.zeros((3, vec_out.shape[1]), F32)
    unit1, inv1 = unit_norm(tok[...].astype(F32))
    first = (unit1 * vec[0:1] + vec[1:2]).astype(BF)
    n1[...] = jnp.zeros_like(n1)

    def step(t, carry):
        weights = wall[t]
        qkv = qkv_ref[t]
        mixed_grad = nn(branch, weights[:, 3 * heads :]).astype(BF)
        triple = []
        for i in range(rows // SEQ_PAD):
            here = slice(i * SEQ_PAD, (i + 1) * SEQ_PAD)
            part, grad = qkv[here], mixed_grad[here]
            sides = [[], [], []]
            for h in range(heads // HEAD_DIM):
                q, k, v = (part[:, j * heads + h * HEAD_DIM : j * heads + (h + 1) * HEAD_DIM] for j in range(3))
                g = grad[:, h * HEAD_DIM : (h + 1) * HEAD_DIM]
                w = softmax_rows(q, k)
                w_grad = nt(g, v)
                s_grad = (w * (w_grad - jnp.sum(w * w_grad, axis=-1, keepdims=True))).astype(BF)
                sides[0].append((nn(s_grad, k) * (HEAD_DIM**-0.5)).astype(BF))
                sides[1].append((tn(s_grad, q) * (HEAD_DIM**-0.5)).astype(BF))
                sides[2].append(tn(w.astype(BF), g).astype(BF))
            triple.append(jnp.concatenate(sides[0] + sides[1] + sides[2], axis=1))
        triple = jnp.concatenate(triple, axis=0)
        dw_out[t] = jnp.concatenate([tn(first, triple), tn(branch, mixed_ref[t])], axis=1).astype(BF)
        n1[...] += nt(triple, weights[:, : 3 * heads])
        sums = jnp.sum(triple.astype(F32), axis=0, keepdims=True)
        bias_out[t] = jnp.broadcast_to(sums, (8, 3 * heads))
        return carry

    lax.fori_loop(0, 4, step, 0)
    grad = n1[...]
    vec_out[0:1] = jnp.sum(grad * unit1, axis=0, keepdims=True)
    vec_out[1:2] = jnp.sum(grad, axis=0, keepdims=True)
    scaled = grad * vec[0:1]
    token_grad[...] += inv1 * (
        scaled
        - jnp.mean(scaled, axis=-1, keepdims=True)
        - unit1 * jnp.mean(scaled * unit1, axis=-1, keepdims=True)
    )


def reduce_kernel(cells, with_small, *refs):
    if with_small:
        e_src, a_src, small, e_out, a_out, small_all, *refs = refs
    else:
        e_src, a_src, e_out, a_out, *refs = refs
    (e_core, a_core, e_own, a_own, e_mid, a_mid, e_side, a_side, e_fin, a_fin, a_in,
     c_s, c_r, y_s, y_r, z_s, z_r, own, *small_sems) = refs
    d, cell, t = place(cells)
    core, side, far = tensor_peers(t)
    here = d * cells + cell

    def at_dp(k):
        return (lax.rem(d + k, 8) * cells + cell, t)

    barrier = pltpu.get_barrier_semaphore()
    if with_small:
        others = [
            (lax.rem(d + k, 8), lax.rem(t + m, 4)) for k in range(8) for m in range(4) if k or m
        ]
        for other in others:
            signal(barrier, other)
        pl.semaphore_wait(barrier, 31)
    else:
        for k in range(1, 8):
            signal(barrier, at_dp(k))
        signal(barrier, (here, core))
        signal(barrier, (here, side))
        pl.semaphore_wait(barrier, 9)

    waits = []
    if with_small:
        s_s, s_r = small_sems
        row = d * 4 + t
        for n, other in enumerate(others):
            copy = remote(small.at[other[0] * 4 + other[1]], small_all.at[row], s_s.at[n], s_r.at[n], other)
            copy.start()
            waits.append(copy)
        small_own = pltpu.make_async_copy(small.at[row], small_all.at[row], own.at[4])
        small_own.start()

    sets = ((e_src, e_core, e_own, e_mid, e_side, e_fin), (a_src, a_core, a_own, a_mid, a_side, a_fin))
    first = {}
    for a, (src, inbox, kept, _, _, _) in enumerate(sets):
        for i, tt in enumerate((far, core)):
            copy = remote(src.at[tt], inbox.at[i], c_s.at[a, i], c_r.at[a, i], (here, core))
            copy.start()
            first[a, i] = copy
        for i, tt in enumerate((side, t)):
            copy = pltpu.make_async_copy(src.at[tt], kept.at[i], own.at[2 * a + i])
            copy.start()
            first[a, 2 + i] = copy
    second = {}
    for a, (_, inbox, kept, mid, arrived, _) in enumerate(sets):
        first[a, 2].wait()
        first[a, 0].wait_recv()
        for k in range(1, 9):
            p = lax.rem(d + k, 8)
            mid[p] = (kept[0, p].astype(F32) + inbox[0, p].astype(F32)).astype(BF)
            copy = remote(mid.at[p], arrived.at[p], y_s.at[a, k - 1], y_r.at[a, k - 1], (here, side))
            copy.start()
            second[a, k] = copy
    for a, (_, inbox, kept, _, arrived, final) in enumerate(sets):
        first[a, 3].wait()
        first[a, 1].wait_recv()
        for k in range(1, 9):
            p = lax.rem(d + k, 8)
            second[a, k].wait_recv()
            total = kept[1, p].astype(F32) + inbox[1, p].astype(F32) + arrived[p].astype(F32)
            final[p] = total.astype(BF)
            target = e_out if a == 0 else a_in
            if k < 8:
                copy = remote(final.at[p], target.at[d], z_s.at[a, k], z_r.at[a, k], at_dp(k))
                copy.start()
                waits.append(copy)
            elif a == 0:
                e_keep = pltpu.make_async_copy(final.at[p], target.at[d], own.at[5])
                e_keep.start()
            else:
                a_in[d] = final[p]
    for copy in waits:
        copy.wait()
    e_keep.wait()
    total = a_in[0].astype(F32)
    for p in range(1, 8):
        total = total + a_in[p].astype(F32)
    a_out[...] = total
    if with_small:
        small_own.wait()
    for a in range(2):
        for i in range(2):
            first[a, i].wait_send()
        for k in range(1, 9):
            second[a, k].wait_send()


def reduce_grads(cells, expert, attn, small):
    with_small = small is not None
    dma = pltpu.SemaphoreType.DMA
    e_block, a_block = expert.shape[1:], attn.shape[1:]
    scratch = []
    for lead in ((2,), (2,), (), (), ()):
        scratch.append(pltpu.VMEM(lead + e_block, BF))
        scratch.append(pltpu.VMEM(lead + a_block, BF))
    scratch.append(pltpu.VMEM(a_block, BF))
    scratch += [dma((2, 2)), dma((2, 2)), dma((2, 8)), dma((2, 8)), dma((2, 8)), dma((2, 8)), dma((6,))]
    shapes = [jax.ShapeDtypeStruct(e_block, BF), jax.ShapeDtypeStruct(a_block[1:], F32)]
    ins, in_specs, out_specs = [expert, attn], [HB, HB], [HB, VM]
    if with_small:
        scratch += [dma((31,)), dma((31,))]
        ins.append(small)
        in_specs.append(HB)
        out_specs.append(HB)
        shapes.append(jax.ShapeDtypeStruct(small.shape, F32))
    return pl.pallas_call(
        functools.partial(reduce_kernel, cells, with_small),
        out_shape=shapes,
        in_specs=in_specs,
        out_specs=out_specs,
        scratch_shapes=scratch,
        compiler_params=pltpu.CompilerParams(
            collective_id=3, has_side_effects=True, vmem_limit_bytes=VMEM_LIMIT
        ),
        name="reduce_grads",
    )(*ins)


def pad_images(rows, fill=0):
    images = rows.reshape((-1, SEQ) + rows.shape[1:])
    spare = [(0, 0), (0, SEQ_PAD - SEQ)] + [(0, 0)] * (rows.ndim - 1)
    return jnp.pad(images, spare, constant_values=fill).reshape((-1,) + rows.shape[1:])


def drop_pad(rows):
    return rows.reshape((-1, SEQ_PAD) + rows.shape[1:])[:, :SEQ].reshape((-1,) + rows.shape[1:])


def body(
    tokens, ln1_gain, ln1_shift, qkv_weight, qv_bias, out_weight, out_bias, ln2_gain, ln2_shift,
    router_weight, expert_in, expert_in_bias, expert_out, expert_out_bias, expert_ids, expert_slots,
    cotangent,
):
    n_dp = lax.axis_size("dp")
    cells = n_dp // 8
    n_all = n_dp * 4
    width = tokens.shape[1]
    experts = expert_in.shape[0]
    piece = ln1_gain.shape[0]
    head_cols = qkv_weight.shape[2]
    ff_slice = expert_in.shape[2]
    ff_piece = expert_in_bias.shape[1]
    index = lax.axis_index("dp")
    d = index // cells
    cell = index % cells
    groups = [[row * cells + c for row in range(8)] for c in range(cells)]
    peers = [[row * cells + c for c in range(cells)] for row in range(8)]

    packed = jnp.concatenate([qkv_weight.reshape(-1, 3 * head_cols), out_weight.T], axis=1)
    expert_pack = jnp.stack([expert_in, jnp.swapaxes(expert_out, 1, 2)], axis=1)
    if cells > 1:
        packed = lax.all_gather(packed, "dp", axis=0, tiled=True, axis_index_groups=peers)
        expert_pack = lax.all_gather(expert_pack, "dp", axis=2, tiled=True, axis_index_groups=peers)
    low_rows = [ln1_gain, ln1_shift, ln2_gain, ln2_shift, out_bias, qv_bias[0], qv_bias[1]]
    small = jnp.concatenate(
        [row.reshape(-1) for row in low_rows]
        + [router_weight.T.reshape(-1), expert_out_bias.reshape(-1), expert_in_bias.reshape(-1)]
    )
    count = small.shape[0]
    tok = pad_images(tokens)
    cot = pad_images(cotangent)
    if cells > 1:
        small_all = lax.all_gather(small, ("dp", "tensor"), axis=0, tiled=False)
        wall, expert_all, cot_all = gather_weights(cells, [packed], expert_pack, cot)
    else:
        block = jnp.pad(small, (0, 2048 - count)).reshape(16, 128)
        wall, small_all, expert_all, cot_all = gather_weights(cells, [packed, block], expert_pack, cot)
        small_all = jnp.swapaxes(small_all, 0, 1).reshape(n_all, 2048)[:, :count]
    lines = 7 + 2 * experts
    lined = small_all[:, : lines * piece].reshape(n_all, lines, piece)
    lined = jnp.swapaxes(lined, 0, 1).reshape(lines, width)
    vec = lined[:8].astype(F32)
    router = lined[7 : 7 + experts]
    down_bias = lax.dynamic_slice_in_dim(lined, 7 + experts + d, 1, 0).astype(F32)
    up_bias = small_all[:, lines * piece :].reshape(n_all, experts, ff_piece)
    up_bias = lax.dynamic_index_in_dim(up_bias, d, 1, keepdims=False).astype(F32)
    up_bias = up_bias.reshape(4, 1, ff_slice)
    biases = vec[5:7].reshape(2, 4, head_cols)
    qkv_bias = jnp.concatenate([biases[0], jnp.zeros_like(biases[0]), biases[1]], axis=1)[:, None, :]
    wall = wall.reshape(4, width, -1)

    ids, places = expert_ids, expert_slots
    labels = jnp.arange(experts, dtype=jnp.int32)
    table = jnp.where(
        ids[:, 0:1] == labels, places[:, 0:1], jnp.where(ids[:, 1:2] == labels, places[:, 1:2], -1)
    )
    table = pad_images(table, -1)
    rows = tok.shape[0]
    table = table.reshape(4, rows, experts)
    table_t = jnp.swapaxes(table, 1, 2)
    t = lax.axis_index("tensor")
    table_own = lax.dynamic_index_in_dim(table_t, t, 0, keepdims=False)

    limit = pltpu.CompilerParams(vmem_limit_bytes=VMEM_LIMIT)
    second, hidden, probs, qkv, mixed = pl.pallas_call(
        attention_kernel,
        out_shape=[
            jax.ShapeDtypeStruct((rows, width), BF),
            jax.ShapeDtypeStruct((rows, width), F32),
            jax.ShapeDtypeStruct((experts, rows), F32),
            jax.ShapeDtypeStruct((4, rows, 3 * head_cols), BF),
            jax.ShapeDtypeStruct((4, rows, head_cols), BF),
        ],
        in_specs=[VM] * 5,
        out_specs=[VM] * 5,
        scratch_shapes=[pltpu.VMEM((rows, width), F32)],
        compiler_params=limit,
        name="attention",
    )(tok, vec, qkv_bias, router, wall)

    dma = pltpu.SemaphoreType.DMA
    slot_shape = jax.ShapeDtypeStruct((2, CAP_PAD, width), BF)
    x_rows, g_rows, probs_all = pl.pallas_call(
        functools.partial(dispatch_kernel, cells),
        out_shape=[slot_shape, slot_shape, jax.ShapeDtypeStruct((4, experts, rows), F32)],
        in_specs=[VM] * 4,
        out_specs=[HB, HB, VM],
        scratch_shapes=[
            pltpu.VMEM((4, rows, width), BF),
            pltpu.VMEM((2, CAP_PAD, width), BF),
            pltpu.VMEM((2, CAP_PAD, width), BF),
            pltpu.VMEM((2, CAP_PAD, width), BF),
            dma((2, 3)), dma((2, 3)), dma((2, 2)), dma((2, 2)), dma((2,)),
        ],
        compiler_params=pltpu.CompilerParams(
            collective_id=1, has_side_effects=True, vmem_limit_bytes=VMEM_LIMIT
        ),
        name="dispatch",
    )(second, probs, table_t, cot_all)

    slots = 2 * CAP_PAD
    fixed = pl.BlockSpec((slots, width), lambda i: (0, 0))
    y_rows, b_rows, q_rows, expert_grad, up_grad, down_grad = pl.pallas_call(
        expert_kernel,
        out_shape=[
            jax.ShapeDtypeStruct((slots, width), BF),
            jax.ShapeDtypeStruct((slots, width), BF),
            jax.ShapeDtypeStruct((2, 8, CAP_PAD), F32),
            jax.ShapeDtypeStruct(expert_all.shape, BF),
            jax.ShapeDtypeStruct((4, 1, ff_slice), F32),
            jax.ShapeDtypeStruct((1, width), F32),
        ],
        grid=(4,),
        in_specs=[
            fixed,
            fixed,
            pl.BlockSpec((1,) + expert_all.shape[1:], lambda i: (i, 0, 0, 0, 0)),
            pl.BlockSpec((1, 1, ff_slice), lambda i: (i, 0, 0)),
            pl.BlockSpec((1, width), lambda i: (0, 0)),
        ],
        out_specs=[
            fixed,
            fixed,
            pl.BlockSpec((2, 8, CAP_PAD), lambda i: (0, 0, 0)),
            pl.BlockSpec((1,) + expert_all.shape[1:], lambda i: (i, 0, 0, 0, 0)),
            pl.BlockSpec((1, 1, ff_slice), lambda i: (i, 0, 0)),
            pl.BlockSpec((1, width), lambda i: (0, 0)),
        ],
        scratch_shapes=[
            pltpu.VMEM((slots, width), F32),
            pltpu.VMEM((slots, width), F32),
            pltpu.VMEM((width, slots), BF),
            pltpu.VMEM((width, slots), BF),
            pltpu.VMEM((slots, ff_slice), BF),
            pltpu.VMEM((slots, ff_slice), BF),
        ],
        compiler_params=limit,
        name="experts",
    )(x_rows.reshape(slots, width), g_rows.reshape(slots, width), expert_all, up_bias, down_bias)

    r_rows, m_rows, q_all = pl.pallas_call(
        functools.partial(combine_kernel, cells),
        out_shape=[
            jax.ShapeDtypeStruct((rows, width), F32),
            jax.ShapeDtypeStruct((rows, width), F32),
            jax.ShapeDtypeStruct((8, 8, CAP_PAD), F32),
        ],
        in_specs=[HB, HB, HB, VM, VM],
        out_specs=[VM, VM, VM],
        scratch_shapes=[
            pltpu.VMEM((2, CAP_PAD, width), BF),
            pltpu.VMEM((2, CAP_PAD, width), BF),
            pltpu.VMEM((2, 2, rows, width), BF),
            pltpu.VMEM((2, 2, rows, width), BF),
            pltpu.VMEM((2, rows, width), BF),
            pltpu.VMEM((2, rows, width), BF),
            dma((2, 2)), dma((2, 2)), dma((2, 4)), dma((8,)), dma((2,)), dma((2,)), dma((1,)), dma((1,)), dma((3,)),
        ],
        compiler_params=pltpu.CompilerParams(
            collective_id=2, has_side_effects=True, vmem_limit_bytes=VMEM_LIMIT
        ),
        name="combine",
    )(
        b_rows.reshape(2, CAP_PAD, width),
        y_rows.reshape(2, CAP_PAD, width),
        q_rows,
        table.astype(F32),
        jnp.swapaxes(probs_all, 1, 2),
    )

    out, token_grad, attn_grad, vec_grad, bias_grad = pl.pallas_call(
        backward_kernel,
        out_shape=[
            jax.ShapeDtypeStruct((rows, width), BF),
            jax.ShapeDtypeStruct((rows, width), F32),
            jax.ShapeDtypeStruct(wall.shape, BF),
            jax.ShapeDtypeStruct((16, width), F32),
            jax.ShapeDtypeStruct((4, 8, 3 * head_cols), F32),
        ],
        in_specs=[VM] * 13,
        out_specs=[VM] * 5,
        scratch_shapes=[pltpu.VMEM((rows, width), F32)],
        compiler_params=limit,
        name="backward",
    )(tok, hidden, r_rows, m_rows, cot, probs, q_all, table_own, router, vec, wall, qkv, mixed)

    bias_grad = bias_grad[:, 0].reshape(4, 3, head_cols)
    pair = jnp.stack([bias_grad[:, 0].reshape(-1), bias_grad[:, 2].reshape(-1)], axis=0)
    small_grad = jnp.concatenate([vec_grad[:5], pair, vec_grad[8:16]], axis=0)
    lines = small_grad.shape[0]
    attn_grad = attn_grad.reshape((4, 8, width // 8) + attn_grad.shape[2:])
    if cells > 1:
        expert_out_grad, attn_part = reduce_grads(cells, expert_grad, attn_grad, None)
        expert_sum = lax.psum_scatter(
            expert_out_grad.astype(F32), "dp", scatter_dimension=2, tiled=True, axis_index_groups=peers
        )
        attn_sum = lax.psum_scatter(attn_part, "dp", scatter_dimension=0, tiled=True, axis_index_groups=peers)
        hot = (labels == d).astype(F32)
        whole = lax.psum(
            (small_grad, hot[:, None] * up_grad.reshape(1, -1), hot[:, None] * down_grad), ("dp", "tensor")
        )
        spot = index * 4 + t
        params = lax.dynamic_slice_in_dim(whole[0], spot * piece, piece, 1)
        up_sum = lax.dynamic_slice_in_dim(whole[1], spot * ff_piece, ff_piece, 1)
        down_sum = lax.dynamic_slice_in_dim(whole[2], spot * piece, piece, 1)
    else:
        message = jnp.concatenate(
            [
                jnp.swapaxes(small_grad.reshape(lines, n_all, piece), 0, 1).reshape(n_all, -1),
                up_grad.reshape(n_all, ff_piece),
                down_grad.reshape(n_all, piece),
            ],
            axis=1,
        )
        message = jnp.pad(message, ((0, 0), (0, 1024 - message.shape[1]))).reshape(n_all, 8, 128)
        expert_sum, attn_sum, small_in = reduce_grads(cells, expert_grad, attn_grad, message)
        small_in = jnp.sum(small_in.reshape(8, 4, 1024), axis=1)
        params = jnp.sum(small_in, axis=0)[: lines * piece].reshape(lines, piece)
        up_sum = small_in[:, lines * piece : lines * piece + ff_piece]
        down_sum = small_in[:, lines * piece + ff_piece : lines * piece + ff_piece + piece]
    return (
        drop_pad(out),
        drop_pad(token_grad),
        params[0],
        params[1],
        attn_sum[:, : 3 * head_cols].reshape(-1, 3, head_cols),
        params[5:7],
        attn_sum[:, 3 * head_cols :].T,
        params[4],
        params[2],
        params[3],
        params[7:15].T,
        expert_sum[:, 0].astype(F32),
        up_sum,
        jnp.swapaxes(expert_sum[:, 1], 1, 2).astype(F32),
        down_sum,
    )


def solution(mesh):
    both = ("dp", "tensor")
    return jax.shard_map(
        body,
        mesh=mesh,
        in_specs=(
            P(both, None),
            P(both),
            P(both),
            P("dp", None, "tensor"),
            P(None, both),
            P("tensor", "dp"),
            P(both),
            P(both),
            P(both),
            P(both, None),
            P(None, "dp", "tensor"),
            P(None, both),
            P(None, "tensor", "dp"),
            P(None, both),
            P("dp", None),
            P("dp", None),
            P(both, None),
        ),
        out_specs=(
            P(both, None),
            P(both, None),
            P(both),
            P(both),
            P("dp", None, "tensor"),
            P(None, both),
            P("tensor", "dp"),
            P(both),
            P(both),
            P(both),
            P(both, None),
            P(None, "dp", "tensor"),
            P(None, both),
            P(None, "tensor", "dp"),
            P(None, both),
        ),
        check_vma=False,
    )
```

time: 1920 us -> 698 us (0.36)
  waiting for transfers between devices: 851 us -> 0 us
  Pallas kernels: 0 us -> 652 us
  blocking collectives: 358 us -> 0 us
  local copies, waits for them, and re-layouts: 321 us -> 31 us
  matrix products: 227 us -> 0 us
  other arithmetic: 118 us -> 8.35 us
  starting transfers between devices: 22.8 us -> 0 us
    reduce_scatter x3 -> x0, waiting for transfers between devices: 704 us -> none  [the longest x1 318 us: body(): lax.psum_scatter(expert_summed[1], 'dp', scatter_dimension=2, tiled=True)]
    pallas_call x0 -> x7, Pallas kernels: none -> 652 us  [the longest x1 152 us: body(): pl.pallas_call(functools.partial(dispatch_kernel, cells), out_shape=[slot...]
    dot_general x25 -> x0, matrix products: 223 us -> none  [the longest x1 49.7 us: body(): jnp.einsum('ecd,efd->ecf', slot_grad, down_used, preferred_element_type=j...]
    all_gather x6 -> x0, blocking collectives: 206 us -> none  [the longest x1 39.6 us: body(): lax.all_gather(qv_bias, ('dp', 'tensor'), axis=1, tiled=True)]
    unnamed x5 -> x0, blocking collectives: 152 us -> none
    unnamed x20 -> x0, waiting for transfers between devices: 132 us -> none
    reduce_sum x12 -> x2, other arithmetic: 67.5 us -> 0.11 us  [the longest x1 0.08 us: body(): small_in = jnp.sum(small_in.reshape(8, 4, 1024), axis=1)]
    gather x4 -> x0, local copies, waits for them, and re-layouts: 61 us -> none  [the longest x2 30.5 us: body(): back_padded[picks]]
  transfers between devices with their start and end apart: 17 -> 0, of which waited for: 8 -> 0; matrix products, arithmetic and copies ran while one was open for 30% -> 0% of each run, Pallas kernels for 0% -> 0%
where the time goes in v1:
time: 698 us; the launch traced here: 693 us
  Pallas kernels  652 us (93%)
  local copies, waits for them, and re-layouts  31 us (4%)
  other arithmetic  8.35 us (1%)
    pallas_call x1, Pallas kernels, body(): pl.pallas_call(functools.partial(dispatch_kernel, cells), out_shape=[slot...  152 us
    pallas_call x1, Pallas kernels, body(): pl.pallas_call(functools.partial(combine_kernel, cells), out_shape=[jax.S...  151 us
    pallas_call x1, Pallas kernels, reduce_grads(): pl.pallas_call(functools.partial(reduce_kernel, cells, with_small), out_s...  131 us
    pallas_call x1, Pallas kernels, gather_weights(): pl.pallas_call(functools.partial(gather_kernel, cells, len(shared)), out_...  119 us
    pallas_call x1, Pallas kernels, body(): pl.pallas_call(expert_kernel, out_shape=[jax.ShapeDtypeStruct((slots, wid...  52.9 us
    pallas_call x1, Pallas kernels, body(): pl.pallas_call(backward_kernel, out_shape=[jax.ShapeDtypeStruct((rows, wi...  32.7 us

profile of v1, /device:TPU:11, one launch (start us, length us, event | category | flops | bytes accessed | tf_op | source)
XLA Modules:
  0.0 692.5 jit_solution(7644828356767846549)
XLA Ops:
  0.7 0.8 slice_bitcast_fusion.1
  1.5 0.8 reshape.203
  2.3 0.8 reshape.201
  3.0 0.8 reshape.202
  3.8 3.4 concatenate.25
  7.8 1.2 reshape.205
  9.0 0.9 pad.21
  9.9 1.6 pad_maximum_fusion.refs_2_
  12.0 0.7 pad_maximum_fusion.1.refs_0_
  12.7 118.9 %gather_weights.1 = (bf16[4,8,96,768]{3,2,1,0:T(8,128)(2,1)}, bf16[4,8,16,128]{3,2,1,0:T(8,128)(2,1)}, bf16[4,8,2,96,768]{4,3,2,1,0:T(8,128)(2,1)}, bf16[4,416,768]{2,1,0:T(8,128)(2,1)}) custom-call(bf16[96,768]{1,0:T(8,128)(2,1)} %pad_maximum_fusion.1.refs_0_, bf16[16,128]{1,0:T(8,128)(2,1)} %pad_bitcast_fusion.refs_1_, ...), custom_call_target="tpu_custom_call" | custom-call | tf_op jit(solution)/shard_map/gather_weights/pallas_call | solution.py:167
  131.6 0.9 copy.57
  133.9 0.7 convert_element_type.47.vec
  134.6 0.7 slice.140.router
  135.5 0.9 pad.19
  136.4 13.9 %attention.1 = (bf16[416,768]{1,0:T(8,128)(2,1)}, f32[416,768]{1,0:T(8,128)}, f32[8,416]{1,0:T(8,128)}, bf16[4,416,576]{2,1,0:T(8,128)(2,1)}, bf16[4,416,192]{2,1,0:T(8,128)(2,1)}) custom-call(bf16[416,768]{1,0:T(8,128)(2,1)} %bitcast.61, f32[8,768]{1,0:T(8,128)} %convert_element_type.47.vec, f32[4,1,576]{2,1,0:T(1,128)} %broadcast_in_dim.33.qkv_bias, ...), custom_call_target="tpu_custom_call" | custom-call | tf_op jit(solution)/shard_map/attention/pallas_call | solution.py:812
  151.5 151.5 %dispatch.1 = (bf16[2,640,768]{2,1,0:T(8,128)(2,1)}, bf16[2,640,768]{2,1,0:T(8,128)(2,1)}, f32[4,8,416]{2,1,0:T(8,128)}) custom-call(bf16[416,768]{1,0:T(8,128)(2,1)} %get-tuple-element.47.second, f32[8,416]{1,0:T(8,128)} %get-tuple-element.48.probs, s32[4,8,416]{2,1,0:T(8,128)} %get-tuple-element.131.slots, bf16[4,416,768]{2,1,0:T(8,128)(2,1)} %get-tuple-element.49.cot_all), custom_call_target="tpu_custom_call" | custom-call | tf_op jit(solution)/shard_map/dispatch/pallas_call | solution.py:830
  304.6 0.7 reshape.227.up_bias
  305.3 52.9 %experts.1 = (bf16[1280,768]{1,0:T(8,128)(2,1)}, bf16[1280,768]{1,0:T(8,128)(2,1)}, f32[2,8,640]{2,1,0:T(8,128)}, bf16[4,8,2,96,768]{4,3,2,1,0:T(8,128)(2,1)}, f32[4,1,768]{2,1,0:T(1,128)}, /*index=5*/f32[1,768]{1,0:T(1,128)}) custom-call(bf16[1280,768]{1,0:T(8,128)(2,1)} %bitcast.65, bf16[1280,768]{1,0:T(8,128)(2,1)} %bitcast.66, ...), custom_call_target="tpu_custom_call" | custom-call | tf_op jit(solution)/shard_map/experts/pallas_call | solution.py:850
  358.2 1.2 copy.63
  359.4 1.2 copy.64.slots
  360.6 151.2 %combine.1 = (f32[416,768]{1,0:T(8,128)}, f32[416,768]{1,0:T(8,128)}, f32[8,8,640]{2,1,0:T(8,128)}) custom-call(bf16[2,640,768]{2,1,0:T(8,128)(2,1)} %bitcast.68, bf16[2,640,768]{2,1,0:T(8,128)(2,1)} %bitcast.67, f32[2,8,640]{2,1,0:T(8,128)} %get-tuple-element.55.q_src, f32[4,416,8]{2,1,0:T(8,128)} %copy.64.slots, f32[4,416,8]{2,1,0:T(8,128)} %bitcast.64), custom_call_target="tpu_custom_call" | custom-call | tf_op jit(solution)/shard_map/combine/pallas_call | solution.py:888
  512.5 32.7 %backward.1 = (bf16[416,768]{1,0:T(8,128)(2,1)}, f32[416,768]{1,0:T(8,128)}, bf16[4,768,768]{2,1,0:T(8,128)(2,1)}, f32[16,768]{1,0:T(8,128)}, f32[4,8,576]{2,1,0:T(8,128)}) custom-call(bf16[416,768]{1,0:T(8,128)(2,1)} %bitcast.62, f32[416,768]{1,0:T(8,128)} %get-tuple-element.46.hid, f32[416,768]{1,0:T(8,128)} %get-tuple-element.57.r_ref, ...), custom_call_target="tpu_custom_call" | custom-call | tf_op jit(solution)/shard_map/backward/pallas_call | solution.py:918
  545.2 0.7 slice.152
  546.0 0.7 slice.148
  546.9 0.9 slice_reduce_fusion.2
  548.8 0.7 copy.71
  549.4 130.8 %reduce_grads.1 = (bf16[8,2,96,768]{3,2,1,0:T(8,128)(2,1)}, f32[96,768]{1,0:T(8,128)}, f32[32,8,128]{2,1,0:T(8,128)}) custom-call(bf16[4,8,2,96,768]{4,3,2,1,0:T(8,128)(2,1)} %get-tuple-element.64.refs_0_, bf16[4,8,96,768]{3,2,1,0:T(8,128)(2,1)} %bitcast.63, f32[32,8,128]{2,1,0:T(8,128)} %bitcast.77), custom_call_target="tpu_custom_call" | custom-call | tf_op jit(solution)/shard_map/reduce_grads/pallas_call | solution.py:723
  680.3 4.4 convert_bitcast_fusion
  684.8 0.9 copy.68
  685.8 0.7 copy.69
  690.2 1.1 reshape.219
  691.4 0.9 reshape.217
  (92 shorter events, 10.8 us)
Async XLA Ops:
  0.6 9.3 %copy-start.2 = (bf16[8,96,768]{2,1,0:T(8,128)(2,1)S(1)}, bf16[8,96,768]{2,1,0:T(8,128)(2,1)}, u32[]{:S(2)}) copy-start(bf16[8,96,768]{2,1,0:T(8,128)(2,1)} %param.27) | copy-start | bytes 3538948
  0.7 9.3 %copy-start.1 = (bf16[8,768,96]{1,2,0:T(8,128)(2,1)S(1)}, bf16[8,768,96]{1,2,0:T(8,128)(2,1)}, u32[]{:S(2)}) copy-start(bf16[8,768,96]{1,2,0:T(8,128)(2,1)} %param.29) | copy-start | bytes 3538948
  9.9 1.6 copy-start.7
  9.9 2.0 copy-start.9
  12.7 122.6 %copy-start.3 = (bf16[394,768]{1,0:T(8,128)(2,1)S(1)}, bf16[394,768]{1,0:T(8,128)(2,1)}, u32[]{:S(2)}) copy-start(bf16[394,768]{1,0:T(8,128)(2,1)} %param.17) | copy-start | bytes 1815556
  136.4 13.9 %copy-start.10 = (s32[1576,2]{0,1:T(2,128)S(1)}, s32[1576,2]{0,1:T(2,128)}, u32[]{:S(2)}) copy-start(s32[1576,2]{0,1:T(2,128)} %param.32) | copy-start | bytes 37828
  136.4 14.1 %copy-start.11 = (s32[1576,2]{0,1:T(2,128)S(1)}, s32[1576,2]{0,1:T(2,128)}, u32[]{:S(2)}) copy-start(s32[1576,2]{0,1:T(2,128)} %param.31) | copy-start | bytes 37828
  305.3 52.9 %copy-start.8 = (f32[4,8,416]{2,1,0:T(8,128)S(1)}, f32[4,8,416]{2,1,0:T(8,128)}, u32[]{:S(2)}) copy-start(f32[4,8,416]{2,1,0:T(8,128)} %get-tuple-element.56) | copy-start | bytes 159748
  512.4 36.0 %copy-start.12 = (f32[4,1,768]{2,1,0:T(1,128)S(1)}, f32[4,1,768]{2,1,0:T(1,128)}, u32[]{:S(2)}) copy-start(f32[4,1,768]{2,1,0:T(1,128)} %get-tuple-element.68) | copy-start | bytes 36868
  512.4 36.1 %copy-start.13 = (f32[1,768]{1,0:T(1,128)S(1)}, f32[1,768]{1,0:T(1,128)}, u32[]{:S(2)}) copy-start(f32[1,768]{1,0:T(1,128)} %get-tuple-element.69) | copy-start | bytes 9220
  680.3 4.4 copy-start.6
  680.3 6.3 copy-start.5
  684.6 5.5 copy-start
  690.1 1.2 copy-start.4

commit v2 on v0

v2 whole, which is shorter than its diff:
```python
import functools

import jax
import jax.numpy as jnp
from jax import lax
from jax.experimental import pallas as pl
from jax.experimental.pallas import tpu as pltpu
from jax.sharding import PartitionSpec as P

HEAD_DIM = 64
SEQ = 197
SEQ_PAD = 208
TOP = 2
QUARTER = 160
SLOTS = 8 * QUARTER
EPS = 1e-6
BF = jnp.bfloat16
F32 = jnp.float32
MESH = pl.DeviceIdType.MESH
VMEM_LIMIT = 60 * 1024 * 1024
VM = pl.BlockSpec(memory_space=pltpu.VMEM)
HB = pl.BlockSpec(memory_space=pl.ANY)


def nn(a, b):
    return lax.dot_general(a, b, (((1,), (0,)), ((), ())), preferred_element_type=F32)


def nt(a, b):
    return lax.dot_general(a, b, (((1,), (1,)), ((), ())), preferred_element_type=F32)


def tn(a, b):
    return lax.dot_general(a, b, (((0,), (0,)), ((), ())), preferred_element_type=F32)


def unit_norm(rows):
    centred = rows - jnp.mean(rows, axis=-1, keepdims=True)
    inv = lax.rsqrt(jnp.mean(centred * centred, axis=-1, keepdims=True) + EPS)
    return centred * inv, inv


def place(cells):
    index = lax.axis_index("dp")
    return lax.div(index, cells), lax.rem(index, cells), lax.axis_index("tensor")


def tensor_peers(t):
    core = t + 1 - 2 * lax.rem(t, 2)
    side = lax.rem(t + 2, 4)
    return core, side, lax.rem(core + 2, 4)


def remote(src, dst, send, recv, device):
    return pltpu.make_async_remote_copy(
        src_ref=src, dst_ref=dst, send_sem=send, recv_sem=recv, device_id=device, device_id_type=MESH
    )


def signal(barrier, device):
    pl.semaphore_signal(barrier, inc=1, device_id=device, device_id_type=MESH)


def softmax_rows(q, k):
    scores = nt(q, k) * (HEAD_DIM**-0.5)
    lane = lax.broadcasted_iota(jnp.int32, scores.shape, 1)
    scores = jnp.where(lane < SEQ, scores, -1e30)
    raised = jnp.exp(scores - jnp.max(scores, axis=-1, keepdims=True))
    return raised / jnp.sum(raised, axis=-1, keepdims=True)


def front_kernel(
    cells,
    packed, small_a, small_b, expert, tok, cot, cols, ids,
    hidden_out, probs_out, gates_all, qkv_out, mixed_out, vec_out, wall, b_all, expert_all, x_out, g_out,
    small_all, cot_all, sec_all, x_buf, g_buf, raw, acc, gates, qkv_bias,
    dp_s, dp_r, y_s, y_r, c_s, c_r, f_s, f_r, own, ag_s, ag_r, x_s, x_r,
):
    d, cell, t = place(cells)
    core, side, far = tensor_peers(t)
    here = d * cells + cell
    rows = tok.shape[0]
    srcs = (small_a, packed, small_b, expert)

    def at_dp(k):
        return (lax.rem(d + k, 8) * cells + cell, t)

    def spot(a, tt, s):
        return small_all.at[s, tt] if a == 0 else (None, wall, b_all, expert_all)[a].at[tt, s]

    barrier = pltpu.get_barrier_semaphore()
    for k in range(1, 8):
        signal(barrier, at_dp(k))
    signal(barrier, (here, core))
    signal(barrier, (here, side))
    pl.semaphore_wait(barrier, 9)

    mine = [
        pltpu.make_async_copy(srcs[a].at[d] if a == 3 else srcs[a], spot(a, t, d), own.at[a]) for a in range(4)
    ]
    dp_copies = [
        [
            remote(
                srcs[a].at[lax.rem(d + k, 8)] if a == 3 else srcs[a],
                spot(a, t, d),
                dp_s.at[a, k],
                dp_r.at[a, k],
                at_dp(k),
            )
            for k in range(1, 8)
        ]
        for a in range(4)
    ]
    side_copies = [[None] * 8 for _ in range(4)]
    near_copies = [[None] * 8 for _ in range(4)]
    far_copies = [[None] * 8 for _ in range(4)]

    def launch(a):
        mine[a].start()
        for copy in dp_copies[a]:
            copy.start()

    def spread(a):
        for k in range(8):
            s = lax.rem(d + 8 - k, 8)
            block = spot(a, t, s)
            if k == 0:
                mine[a].wait()
            else:
                dp_copies[a][k - 1].wait_recv()
            side_copies[a][k] = remote(block, block, y_s.at[a, k], y_r.at[a, k], (here, side))
            side_copies[a][k].start()
            near_copies[a][k] = remote(block, block, c_s.at[a, k], c_r.at[a, k], (here, core))
            near_copies[a][k].start()

    def forward(a):
        for k in range(8):
            block = spot(a, side, lax.rem(d + 8 - k, 8))
            side_copies[a][k].wait_recv()
            far_copies[a][k] = remote(block, block, f_s.at[a, k], f_r.at[a, k], (here, core))
            far_copies[a][k].start()

    def arrive(copies):
        for copy in copies:
            copy.wait_recv()

    def exchange(n, src, dst):
        over = remote(src, dst.at[t], ag_s.at[n, 0], ag_r.at[n, 0], (here, side))
        near = remote(src, dst.at[t], ag_s.at[n, 1], ag_r.at[n, 1], (here, core))
        over.start()
        near.start()
        return over, near

    def pass_on(n, pair, dst):
        pair[0].wait_recv()
        along = remote(dst.at[side], dst.at[side], ag_s.at[n, 2], ag_r.at[n, 2], (here, core))
        along.start()
        return pair + (along,)

    launch(0)
    launch(1)
    cot_pair = exchange(0, cot, cot_all)
    cot_all[t] = cot[...]
    spread(0)
    forward(0)
    arrive(near_copies[0])
    arrive(far_copies[0])
    columns = small_all[...].reshape(-1, 128)
    vec = columns.T[:32]
    vec_out[...] = vec
    heads = qkv_out.shape[2] // 3
    for tt in range(4):
        cut = slice(tt * heads, (tt + 1) * heads)
        qkv_bias[tt] = jnp.concatenate([vec[5:6, cut], jnp.zeros((1, heads), F32), vec[6:7, cut]], axis=1)
    inputs = tok[...].astype(F32)
    unit, _ = unit_norm(inputs)
    first = (unit * vec[0:1] + vec[1:2]).astype(BF)
    acc[...] = inputs + vec[4:5]

    def attend(tt):
        weights = wall[tt].reshape(8 * packed.shape[0], -1)
        qkv = (nn(first, weights[:, : 3 * heads]) + qkv_bias[tt]).astype(BF)
        qkv_out[tt] = qkv
        mixed = []
        for i in range(rows // SEQ_PAD):
            part = qkv[i * SEQ_PAD : (i + 1) * SEQ_PAD]
            sides = []
            for h in range(heads // HEAD_DIM):
                q, k, v = (part[:, j * heads + h * HEAD_DIM : j * heads + (h + 1) * HEAD_DIM] for j in range(3))
                sides.append(nn(softmax_rows(q, k).astype(BF), v).astype(BF))
            mixed.append(jnp.concatenate(sides, axis=1))
        mixed = jnp.concatenate(mixed, axis=0)
        mixed_out[tt] = mixed
        acc[...] += nt(mixed, weights[:, 3 * heads :])

    spread(1)
    launch(3)
    launch(2)
    cot_pair = pass_on(0, cot_pair, cot_all)
    attend(t)
    forward(1)
    attend(side)
    arrive(near_copies[1])
    attend(core)
    arrive(far_copies[1])
    attend(far)

    hidden = acc[...]
    hidden_out[...] = hidden
    unit, _ = unit_norm(hidden)
    second = (unit * vec[2:3] + vec[3:4]).astype(BF)
    sec_all[t] = second
    sec_pair = exchange(1, sec_all.at[t], sec_all)
    logits = nt(vec[7:15].astype(BF), second)
    raised = jnp.exp(logits - jnp.max(logits, axis=0, keepdims=True))
    probs = raised / jnp.sum(raised, axis=0, keepdims=True)
    probs_out[...] = probs
    lane = lax.broadcasted_iota(jnp.int32, probs.shape, 0)
    picked = [jnp.sum(jnp.where(lane == ids[k : k + 1], probs, 0.0), axis=0, keepdims=True) for k in range(2)]
    gates[...] = jnp.concatenate(picked + [jnp.zeros((6, rows), F32)], axis=0)
    gates_all[t] = gates[...]
    gate_pair = exchange(2, gates, gates_all)

    pair_rows = 2 * QUARTER

    def onehots(tt, base):
        at = lax.broadcasted_iota(jnp.int32, (pair_rows, rows), 0) + base
        return at == cols[tt, 0:1], at == cols[tt, 1:2]

    def pick(base, source):
        total = None
        for tt in range(4):
            one, two = onehots(tt, base)
            part = nn(jnp.logical_or(one, two).astype(F32).astype(BF), source[tt])
            total = part if total is None else total + part
        return total.astype(BF)

    def chunk(i):
        c = lax.rem(lax.div(d, 2) + 1 + i, 4)
        return c, pl.multiple_of(c * pair_rows, pair_rows)

    arrive([cot_pair[1], cot_pair[2]])
    for i in range(4):
        c, base = chunk(i)
        raw[pl.ds(base, pair_rows)] = pick(base, cot_all)
    sec_pair = pass_on(1, sec_pair, sec_all)
    gate_pair = pass_on(2, gate_pair, gates_all)
    arrive([sec_pair[1], sec_pair[2], gate_pair[1], gate_pair[2]])

    sent = []

    def post(n, i, buf, out):
        c, base = chunk(i)
        for h in range(2):
            e = 2 * c + h
            block = buf.at[pl.ds(pl.multiple_of(base + h * QUARTER, QUARTER), QUARTER)]
            copy = remote(block, out.at[d], x_s.at[n, e], x_r.at[n, d], (e * cells + cell, t))
            keep = pltpu.make_async_copy(block, out.at[d], own.at[4 + n])
            sent.append((e, copy, keep))

            @pl.when(e == d)
            def _():
                keep.start()

            @pl.when(e != d)
            def _():
                copy.start()

    for i in range(4):
        c, base = chunk(i)
        x_buf[pl.ds(base, pair_rows)] = pick(base, sec_all)
        post(0, i, x_buf, x_out)
    for i in range(4):
        c, base = chunk(i)
        gate = None
        for tt in range(4):
            one, two = onehots(tt, base)
            part = jnp.where(one, gates_all[tt, 0:1], jnp.where(two, gates_all[tt, 1:2], 0.0))
            part = jnp.sum(part, axis=1, keepdims=True)
            gate = part if gate is None else gate + part
        here_rows = pl.ds(base, pair_rows)
        g_buf[here_rows] = (gate * raw[here_rows].astype(F32)).astype(BF)
        post(1, i, g_buf, g_out)

    spread(3)
    spread(2)
    forward(3)
    forward(2)
    for a in (2, 3):
        arrive(near_copies[a])
        arrive(far_copies[a])
    for n, (buf, out) in enumerate(((x_buf, x_out), (g_buf, g_out))):
        for k in range(1, 8):
            g = lax.rem(d + 8 - k, 8)
            remote(buf.at[pl.ds(0, QUARTER)], out.at[g], x_s.at[n, g], x_r.at[n, g], at_dp(8 - k)).wait_recv()
    for e, copy, keep in sent:

        @pl.when(e == d)
        def _():
            keep.wait()

        @pl.when(e != d)
        def _():
            copy.wait_send()

    for a in range(4):
        for copy in dp_copies[a] + side_copies[a] + near_copies[a] + far_copies[a]:
            copy.wait_send()
    for trio in (cot_pair, sec_pair, gate_pair):
        for copy in trio:
            copy.wait_send()


def gelu_both(x):
    phi = 0.5 * (1.0 + lax.erf(x * (0.5**0.5)))
    slope = phi + x * (jnp.exp(-0.5 * x * x) * 0.3989422804014327)
    return x * phi, slope


def middle_kernel(
    cells,
    x_ref, g_ref, expert_all, up_bias, vec, cols, gates,
    r_out, m_out, q_out, grad_out, dup_out, ddown_out,
    w_buf, act_buf, pre_buf, x_turned, g_turned, y_acc, b_acc, y_buf, b_buf, q_buf, y_in, b_in, q_in,
    blocks, core_in, side_buf, side_in, q_blocks, q_core, q_side, q_mid,
    load, store, a_s, a_r, q_s, q_r, c_s, c_r, y_s, y_r, own,
):
    d, cell, t = place(cells)
    core, side, far = tensor_peers(t)
    here = d * cells + cell
    width = x_ref.shape[1]
    ff = act_buf.shape[2]
    pair_rows = 2 * QUARTER

    def at_dp(k):
        return (lax.rem(d + k, 8) * cells + cell, t)

    loads = [pltpu.make_async_copy(expert_all.at[tt], w_buf.at[tt], load.at[tt]) for tt in range(4)]
    for copy in loads:
        copy.start()
    barrier = pltpu.get_barrier_semaphore()
    for k in range(1, 8):
        signal(barrier, at_dp(k))
    signal(barrier, (here, core))
    signal(barrier, (here, side))
    pl.semaphore_wait(barrier, 9)

    x_turned[...] = x_ref[...].T
    g_turned[...] = g_ref[...].T
    ddown_out[...] = jnp.sum(g_ref[...].astype(F32), axis=0, keepdims=True)
    dup_out[...] = jnp.zeros_like(dup_out)
    for copy in loads:
        copy.wait()

    def weights(tt):
        return w_buf[tt, :, 0].reshape(width, ff), w_buf[tt, :, 1].reshape(width, ff)

    sent = []

    def post(n, c, buf, out):
        for h in range(2):
            g = 2 * c + h
            block = buf.at[g]
            copy = remote(block, out.at[d], a_s.at[n, g], a_r.at[n, d], (g * cells + cell, t))
            keep = pltpu.make_async_copy(block, out.at[d], own.at[n])
            sent.append((g, copy, keep))

            @pl.when(g == d)
            def _():
                keep.start()

            @pl.when(g != d)
            def _():
                copy.start()

    ones = jnp.ones((8, width), BF)
    for i in range(4):
        c = lax.rem(lax.div(d, 2) + 1 + i, 4)
        rows = pl.ds(pl.multiple_of(c * pair_rows, pair_rows), pair_rows)
        y_acc[...] = jnp.broadcast_to(vec[pl.ds(15 + d, 1)], y_acc.shape)
        b_acc[...] = jnp.zeros_like(b_acc)

        def slice_step(tt, carry):
            w_in, w_out = weights(tt)
            pre = nn(x_ref[rows], w_in) + up_bias[tt]
            act, slope = gelu_both(pre)
            act = act.astype(BF)
            act_buf[tt, rows] = act
            pre_grad = (nn(g_ref[rows], w_out) * slope).astype(BF)
            pre_buf[tt, rows] = pre_grad
            y_acc[...] += nt(act, w_out)
            b_acc[...] += nt(pre_grad, w_in)
            dup_out[tt] += jnp.sum(pre_grad.astype(F32), axis=0, keepdims=True)
            return carry

        lax.fori_loop(0, 4, slice_step, 0)
        y = y_acc[...]
        pair = pl.ds(2 * c, 2)
        b_buf[pair] = b_acc[...].astype(BF).reshape(2, QUARTER, width)
        y_buf[pair] = y.astype(BF).reshape(2, QUARTER, width)
        post(0, c, b_buf, b_in)
        z = y * g_ref[rows].astype(F32)
        high = z.astype(BF)
        low = (z - high.astype(F32)).astype(BF)
        for h in range(2):
            part = slice(h * QUARTER, (h + 1) * QUARTER)
            q_buf[2 * c + h] = nt(ones, high[part]) + nt(ones, low[part])
        post(2, c, q_buf, q_in)
    for i in range(4):
        post(1, lax.rem(lax.div(d, 2) + 1 + i, 4), y_buf, y_in)

    def grad_slice(tt, carry):
        def grad_rows(n, inner):
            span = pl.ds(pl.multiple_of(n * 192, 192), 192)
            pair = pl.ds(2 * n, 2)
            w_buf[tt, pair, 0] = nn(x_turned[span], pre_buf[tt]).astype(BF).reshape(2, width // 8, ff)
            w_buf[tt, pair, 1] = nn(g_turned[span], act_buf[tt]).astype(BF).reshape(2, width // 8, ff)
            return inner

        lax.fori_loop(0, width // 192, grad_rows, 0)
        return carry

    lax.fori_loop(0, 4, grad_slice, 0)
    stores = [pltpu.make_async_copy(w_buf.at[tt], grad_out.at[tt], store.at[tt]) for tt in range(4)]
    for copy in stores:
        copy.start()

    def landed(n, buf, out):
        for k in range(1, 8):
            e = lax.rem(d + 8 - k, 8)
            remote(buf.at[0], out.at[e], a_s.at[n, e], a_r.at[n, e], at_dp(8 - k)).wait_recv()

    def own_landed(n, buf, out):
        pltpu.make_async_copy(buf.at[d], out.at[d], own.at[n]).wait()

    def onehots(tt):
        at = lax.broadcasted_iota(jnp.int32, (cols.shape[1], SLOTS), 1)
        return at == cols[tt, :, 0:1], at == cols[tt, :, 1:2]

    landed(0, b_buf, b_in)
    own_landed(0, b_buf, b_in)
    landed(2, q_buf, q_in)
    own_landed(2, q_buf, q_in)
    q_line = jnp.concatenate([q_in[e] for e in range(8)], axis=1)
    owner = jnp.concatenate([jnp.full((8, QUARTER), e, jnp.int32) for e in range(8)], axis=1)
    q_line = jnp.where(lax.broadcasted_iota(jnp.int32, q_line.shape, 0) == owner, q_line, 0.0)
    q_high = q_line.astype(BF)
    q_both = jnp.concatenate([q_high, (q_line - q_high.astype(F32)).astype(BF)], axis=0)
    b_rows = b_in[...].reshape(SLOTS, width)

    def back_block(tt):
        one, two = onehots(tt)
        hot = jnp.logical_or(one, two).astype(F32).astype(BF)
        q = nt(q_both, hot)
        return nn(hot, b_rows), q[0:8] + q[8:16]

    def out_block(tt):
        one, two = onehots(tt)
        hot = jnp.where(one, gates[tt, :, 0:1], jnp.where(two, gates[tt, :, 1:2], 0.0)).astype(BF)
        return nn(hot, y_in[...].reshape(SLOTS, width))

    def core_send(n, i, src, dst):
        copy = remote(src.at[i], dst.at[i], c_s.at[n, i], c_r.at[n, i], (here, core))
        copy.start()
        return copy

    def side_send(n, src, dst):
        copy = remote(src, dst, y_s.at[n], y_r.at[n], (here, side))
        copy.start()
        return copy

    core_b, core_q = [], []
    for i, tt in enumerate((far, core)):
        total, q = back_block(tt)
        blocks[i] = total.astype(BF)
        q_blocks[i] = q
        core_b.append(core_send(0, i, blocks, core_in.at[0]))
        core_q.append(core_send(2, i, q_blocks, q_core))
    total, q = back_block(side)
    core_b[0].wait_recv()
    core_q[0].wait_recv()
    side_buf[...] = (total + core_in[0, 0].astype(F32)).astype(BF)
    q_mid[...] = q + q_core[0]
    side_b = side_send(0, side_buf, side_in.at[0])
    side_q = side_send(2, q_mid, q_side)
    total, q = back_block(t)
    core_b[1].wait_recv()
    core_q[1].wait_recv()
    r_out[...] = total + core_in[0, 1].astype(F32)
    q_out[...] = q + q_core[1]

    landed(1, y_buf, y_in)
    own_landed(1, y_buf, y_in)
    core_y = []
    for i, tt in enumerate((far, core)):
        core_b[i].wait_send()
        blocks[i] = out_block(tt).astype(BF)
        core_y.append(core_send(1, i, blocks, core_in.at[1]))
    total = out_block(side)
    core_y[0].wait_recv()
    side_b.wait_send()
    side_buf[...] = (total + core_in[1, 0].astype(F32)).astype(BF)
    side_y = side_send(1, side_buf, side_in.at[1])
    total = out_block(t)
    core_y[1].wait_recv()
    total = total + core_in[1, 1].astype(F32)
    side_b.wait_recv()
    side_q.wait_recv()
    r_out[...] += side_in[0].astype(F32)
    q_out[...] += q_side[...]
    side_y.wait_recv()
    m_out[...] = total + side_in[1].astype(F32)

    for copy in core_q + core_y + [side_q, side_y]:
        copy.wait_send()
    for g, copy, keep in sent:

        @pl.when(g != d)
        def _():
            copy.wait_send()

    for copy in stores:
        copy.wait()


def back_kernel(
    cells,
    tok, hid, r_ref, m_ref, cot, probs, picked_ref, vec, wall, qkv_ref, mixed_ref, e_src, bias_msg,
    out, token_grad, e_out, a_out, msg_all, vec_all,
    n1, vec_grad, vec_msg, a_grad, qv_grad,
    e_core, a_core, e_own, e_mid, a_mid, e_side, a_side, e_fin, a_fin, a_in,
    c_s, c_r, y_s, y_r, z_s, z_r, own, m_s, m_r, v_s, v_r,
):
    d, cell, t = place(cells)
    core, side, far = tensor_peers(t)
    here = d * cells + cell
    heads = qkv_ref.shape[2] // 3
    rows = tok.shape[0]
    width = tok.shape[1]
    spot = d * 4 + t

    def at_dp(k):
        return (lax.rem(d + k, 8) * cells + cell, t)

    others = [(k, m) for k in range(8) for m in range(4) if k or m]

    def other(k, m):
        return lax.rem(d + k, 8), lax.rem(t + m, 4)

    barrier = pltpu.get_barrier_semaphore()
    for k, m in others:
        dd, tt = other(k, m)
        signal(barrier, (dd * cells + cell, tt))
    pl.semaphore_wait(barrier, 31)

    waits = []
    first = []
    for i, tt in enumerate((far, core)):
        copy = remote(e_src.at[tt], e_core.at[i], c_s.at[0, i], c_r.at[0, i], (here, core))
        copy.start()
        first.append(copy)
    keeps = []
    for i, tt in enumerate((side, t)):
        copy = pltpu.make_async_copy(e_src.at[tt], e_own.at[i], own.at[i])
        copy.start()
        keeps.append(copy)
    for n, (k, m) in enumerate(others):
        dd, tt = other(k, m)
        copy = remote(bias_msg.at[dd * 4 + tt], msg_all.at[spot], m_s.at[n], m_r.at[n], (dd * cells + cell, tt))
        copy.start()
        waits.append(copy)
    msg_own = pltpu.make_async_copy(bias_msg.at[spot], msg_all.at[spot], own.at[2])
    msg_own.start()

    hidden = hid[...]
    out[...] = (hidden + m_ref[...]).astype(BF)
    picked = picked_ref[...]
    logit = picked - probs[...] * jnp.sum(picked, axis=0, keepdims=True)
    high = logit.astype(BF)
    both = jnp.concatenate([high, (logit - high.astype(F32)).astype(BF)], axis=0)
    unit, inv = unit_norm(hidden)
    gain = vec[2:3]
    second = (unit * gain + vec[3:4]).astype(BF)
    router_grad = nn(both, second)
    vec_grad[...] = jnp.zeros_like(vec_grad)
    vec_grad[8:16] = router_grad[0:8] + router_grad[8:16]
    table = vec[7:15].astype(BF)
    n2 = r_ref[...] + tn(both, jnp.concatenate([table, table], axis=0))
    vec_grad[2:3] = jnp.sum(n2 * unit, axis=0, keepdims=True)
    vec_grad[3:4] = jnp.sum(n2, axis=0, keepdims=True)
    scaled = n2 * gain
    back = inv * (
        scaled
        - jnp.mean(scaled, axis=-1, keepdims=True)
        - unit * jnp.mean(scaled * unit, axis=-1, keepdims=True)
    )
    hidden_grad = cot[...].astype(F32) + back
    token_grad[...] = hidden_grad
    branch = hidden_grad.astype(BF)
    vec_grad[4:5] = jnp.sum(branch.astype(F32), axis=0, keepdims=True)
    unit1, inv1 = unit_norm(tok[...].astype(F32))
    first_norm = (unit1 * vec[0:1] + vec[1:2]).astype(BF)
    n1[...] = jnp.zeros_like(n1)

    second_e = {}
    keeps[0].wait()
    first[0].wait_recv()
    for k in range(1, 9):
        p = lax.rem(d + k, 8)
        e_mid[p] = (e_own[0, p].astype(F32) + e_core[0, p].astype(F32)).astype(BF)
        copy = remote(e_mid.at[p], e_side.at[p], y_s.at[0, k - 1], y_r.at[0, k - 1], (here, side))
        copy.start()
        second_e[k] = copy
    keeps[1].wait()
    first[1].wait_recv()

    def finish_expert(k):
        p = lax.rem(d + k, 8)
        second_e[k].wait_recv()
        total = e_own[1, p].astype(F32) + e_core[1, p].astype(F32) + e_side[p].astype(F32)
        e_fin[p] = total.astype(BF)
        if k < 8:
            copy = remote(e_fin.at[p], e_out.at[d], z_s.at[0, k], z_r.at[0, k], at_dp(k))
            copy.start()
            waits.append(copy)

    def attend_back(tt):
        weights = wall[tt].reshape(width, -1)
        qkv = qkv_ref[tt]
        mixed_grad = nn(branch, weights[:, 3 * heads :]).astype(BF)
        triple = []
        for i in range(rows // SEQ_PAD):
            span = slice(i * SEQ_PAD, (i + 1) * SEQ_PAD)
            part, grad = qkv[span], mixed_grad[span]
            sides = [[], [], []]
            for h in range(heads // HEAD_DIM):
                q, k, v = (part[:, j * heads + h * HEAD_DIM : j * heads + (h + 1) * HEAD_DIM] for j in range(3))
                g = grad[:, h * HEAD_DIM : (h + 1) * HEAD_DIM]
                w = softmax_rows(q, k)
                w_grad = nt(g, v)
                s_grad = (w * (w_grad - jnp.sum(w * w_grad, axis=-1, keepdims=True))).astype(BF)
                sides[0].append((nn(s_grad, k) * (HEAD_DIM**-0.5)).astype(BF))
                sides[1].append((tn(s_grad, q) * (HEAD_DIM**-0.5)).astype(BF))
                sides[2].append(tn(w.astype(BF), g).astype(BF))
            triple.append(jnp.concatenate(sides[0] + sides[1] + sides[2], axis=1))
        triple = jnp.concatenate(triple, axis=0)
        grad = jnp.concatenate([tn(first_norm, triple), tn(branch, mixed_ref[tt])], axis=1).astype(BF)
        a_grad[tt] = grad.reshape(8, width // 8, -1)
        n1[...] += nt(triple, weights[:, : 3 * heads])
        sums = jnp.sum(triple.astype(F32), axis=0, keepdims=True)
        qv_grad[tt] = sums

    core_a = []
    for i, tt in enumerate((far, core)):
        attend_back(tt)
        copy = remote(a_grad.at[tt], a_core.at[i], c_s.at[1, i], c_r.at[1, i], (here, core))
        copy.start()
        core_a.append(copy)
        finish_expert(2 * i + 1)
        finish_expert(2 * i + 2)
    attend_back(side)
    core_a[0].wait_recv()
    second_a = {}
    for k in range(1, 9):
        p = lax.rem(d + k, 8)
        a_mid[p] = (a_grad[side, p].astype(F32) + a_core[0, p].astype(F32)).astype(BF)
        copy = remote(a_mid.at[p], a_side.at[p], y_s.at[1, k - 1], y_r.at[1, k - 1], (here, side))
        copy.start()
        second_a[k] = copy
    finish_expert(5)
    finish_expert(6)
    attend_back(t)
    finish_expert(7)
    finish_expert(8)
    e_keep = pltpu.make_async_copy(e_fin.at[d], e_out.at[d], own.at[3])
    e_keep.start()
    core_a[1].wait_recv()
    for k in range(1, 9):
        p = lax.rem(d + k, 8)
        second_a[k].wait_recv()
        total = a_grad[t, p].astype(F32) + a_core[1, p].astype(F32) + a_side[p].astype(F32)
        if k < 8:
            a_fin[p] = total.astype(BF)
            copy = remote(a_fin.at[p], a_in.at[d], z_s.at[1, k], z_r.at[1, k], at_dp(k))
            copy.start()
            waits.append(copy)
        else:
            a_out[...] = total

    grad = n1[...]
    vec_grad[0:1] = jnp.sum(grad * unit1, axis=0, keepdims=True)
    vec_grad[1:2] = jnp.sum(grad, axis=0, keepdims=True)
    for j, row in ((0, 5), (2, 6)):
        parts = [qv_grad[tt][:, j * heads : (j + 1) * heads] for tt in range(4)]
        vec_grad[row : row + 1] = jnp.concatenate(parts, axis=1)
    turned = vec_grad[...].T
    vec_msg[...] = turned.reshape(vec_msg.shape)
    for n, (k, m) in enumerate(others):
        dd, tt = other(k, m)
        copy = remote(vec_msg.at[dd * 4 + tt], vec_all.at[spot], v_s.at[n], v_r.at[n], (dd * cells + cell, tt))
        copy.start()
        waits.append(copy)
    vec_all[spot] = vec_msg[spot]
    scaled = grad * vec[0:1]
    token_grad[...] += inv1 * (
        scaled
        - jnp.mean(scaled, axis=-1, keepdims=True)
        - unit1 * jnp.mean(scaled * unit1, axis=-1, keepdims=True)
    )
    for copy in waits:
        copy.wait()
    for k in range(1, 8):
        a_out[...] += a_in[lax.rem(d + k, 8)].astype(F32)
    e_keep.wait()
    msg_own.wait()
    for copy in first + core_a:
        copy.wait_send()
    for k in range(1, 9):
        second_e[k].wait_send()
        second_a[k].wait_send()


def pad_images(rows, fill=0):
    images = rows.reshape((-1, SEQ) + rows.shape[1:])
    spare = [(0, 0), (0, SEQ_PAD - SEQ)] + [(0, 0)] * (rows.ndim - 1)
    return jnp.pad(images, spare, constant_values=fill).reshape((-1,) + rows.shape[1:])


def drop_pad(rows):
    return rows.reshape((-1, SEQ_PAD) + rows.shape[1:])[:, :SEQ].reshape((-1,) + rows.shape[1:])


def body(
    tokens, ln1_gain, ln1_shift, qkv_weight, qv_bias, out_weight, out_bias, ln2_gain, ln2_shift,
    router_weight, expert_in, expert_in_bias, expert_out, expert_out_bias, expert_ids, expert_slots,
    cotangent,
):
    n_dp = lax.axis_size("dp")
    cells = n_dp // 8
    width = tokens.shape[1]
    experts = expert_in.shape[0]
    head_cols = qkv_weight.shape[2]
    ff_slice = expert_in.shape[2]
    index = lax.axis_index("dp")
    t = lax.axis_index("tensor")
    d, cell = index // cells, index % cells
    peers = [[row * cells + c for c in range(cells)] for row in range(8)]

    packed = jnp.concatenate([qkv_weight.reshape(-1, 3 * head_cols), out_weight.T], axis=1)
    expert_pack = jnp.stack([expert_in, jnp.swapaxes(expert_out, 1, 2)], axis=1)
    lines = [ln1_gain, ln1_shift, ln2_gain, ln2_shift, out_bias, qv_bias[0], qv_bias[1]]
    small_a = jnp.concatenate([jnp.stack(lines, axis=1), router_weight, expert_out_bias.T], axis=1)
    small_b = expert_in_bias
    if cells > 1:
        packed = lax.all_gather(packed, "dp", axis=0, tiled=True, axis_index_groups=peers)
        expert_pack = lax.all_gather(expert_pack, "dp", axis=2, tiled=True, axis_index_groups=peers)

        def quarter(piece, axis):
            piece = lax.all_gather(piece, "tensor", axis=axis, tiled=True)
            piece = lax.all_gather(piece, "dp", axis=axis, tiled=True, axis_index_groups=peers)
            size = piece.shape[axis] // 4
            return lax.dynamic_slice_in_dim(piece, t * size, size, axis)

        small_a, small_b = quarter(small_a, 0), quarter(small_b, 1)
    piece, ff_piece = small_a.shape[0], small_b.shape[1]
    small_a = jnp.pad(small_a.astype(F32), ((0, 0), (0, 128 - small_a.shape[1])))
    small_b = jnp.pad(small_b, ((0, 16 - experts), (0, 128 - ff_piece)))
    tok = pad_images(tokens)
    cot = pad_images(cotangent)
    rows = tok.shape[0]

    wanted = expert_slots - QUARTER * t
    inside = jnp.logical_and(expert_slots >= 0, jnp.logical_and(wanted >= 0, wanted < QUARTER))
    cols = jnp.where(inside, expert_ids * QUARTER + wanted, -1)
    cols = jnp.pad(pad_images(cols, -1).reshape(4, rows, TOP), ((0, 0), (0, 0), (0, 8 - TOP)), constant_values=-1)
    cols_t = jnp.swapaxes(cols, 1, 2)
    own_ids = lax.dynamic_slice_in_dim(expert_ids, t * tokens.shape[0], tokens.shape[0], 0)
    ids = jnp.pad(pad_images(own_ids, -1).T, ((0, 8 - TOP), (0, 0)), constant_values=-1)

    dma = pltpu.SemaphoreType.DMA

    def params(identity):
        return pltpu.CompilerParams(
            collective_id=identity, has_side_effects=True, vmem_limit_bytes=VMEM_LIMIT
        )

    def like(shape, dtype=BF):
        return jax.ShapeDtypeStruct(shape, dtype)

    slot_shape = (8, QUARTER, width)
    hidden, probs, gates, qkv, mixed, vec, wall, bias_all, expert_all, x_rows, g_rows = pl.pallas_call(
        functools.partial(front_kernel, cells),
        out_shape=[
            like((rows, width), F32),
            like((experts, rows), F32),
            like((4, 8, rows), F32),
            like((4, rows, 3 * head_cols)),
            like((4, rows, head_cols)),
            like((32, width), F32),
            like((4, 8) + packed.shape),
            like((4, 8) + small_b.shape),
            like((4,) + expert_pack.shape),
            like(slot_shape),
            like(slot_shape),
        ],
        in_specs=[HB] * 4 + [VM] * 4,
        out_specs=[VM] * 7 + [HB] * 4,
        scratch_shapes=[
            pltpu.VMEM((8, 4) + small_a.shape, F32),
            pltpu.VMEM((4, rows, width), BF),
            pltpu.VMEM((4, rows, width), BF),
            pltpu.VMEM((SLOTS, width), BF),
            pltpu.VMEM((SLOTS, width), BF),
            pltpu.VMEM((SLOTS, width), BF),
            pltpu.VMEM((rows, width), F32),
            pltpu.VMEM((8, rows), F32),
            pltpu.VMEM((4, 1, 3 * head_cols), F32),
        ]
        + [dma((4, 8))] * 8
        + [dma((6,)), dma((3, 3)), dma((3, 3)), dma((2, 8)), dma((2, 8))],
        compiler_params=params(0),
        name="front",
    )(packed, small_a, small_b, expert_pack, tok, cot, cols_t, ids)

    bias_all = jnp.swapaxes(bias_all, 0, 1)
    up_bias = lax.dynamic_index_in_dim(bias_all, d, 2, keepdims=False)[:, :, :ff_piece]
    up_bias = up_bias.astype(F32).reshape(4, 1, ff_slice)
    r_rows, m_rows, picked, expert_grad, up_grad, down_grad = pl.pallas_call(
        functools.partial(middle_kernel, cells),
        out_shape=[
            like((rows, width), F32),
            like((rows, width), F32),
            like((8, rows), F32),
            like(expert_all.shape),
            like((4, 1, ff_slice), F32),
            like((1, width), F32),
        ],
        in_specs=[VM, VM, HB, VM, VM, VM, VM],
        out_specs=[VM, VM, VM, HB, VM, VM],
        scratch_shapes=[
            pltpu.VMEM(expert_all.shape, BF),
            pltpu.VMEM((4, SLOTS, ff_slice), BF),
            pltpu.VMEM((4, SLOTS, ff_slice), BF),
            pltpu.VMEM((width, SLOTS), BF),
            pltpu.VMEM((width, SLOTS), BF),
            pltpu.VMEM((2 * QUARTER, width), F32),
            pltpu.VMEM((2 * QUARTER, width), F32),
            pltpu.VMEM(slot_shape, BF),
            pltpu.VMEM(slot_shape, BF),
            pltpu.VMEM((8, 8, QUARTER), F32),
            pltpu.VMEM(slot_shape, BF),
            pltpu.VMEM(slot_shape, BF),
            pltpu.VMEM((8, 8, QUARTER), F32),
            pltpu.VMEM((2, rows, width), BF),
            pltpu.VMEM((2, 2, rows, width), BF),
            pltpu.VMEM((rows, width), BF),
            pltpu.VMEM((2, rows, width), BF),
            pltpu.VMEM((2, 8, rows), F32),
            pltpu.VMEM((2, 8, rows), F32),
            pltpu.VMEM((8, rows), F32),
            pltpu.VMEM((8, rows), F32),
            dma((4,)), dma((4,)), dma((3, 8)), dma((3, 8)), dma((1,)), dma((1,)), dma((3, 2)), dma((3, 2)),
            dma((3,)), dma((3,)), dma((3,)),
        ],
        compiler_params=params(1),
        name="middle",
    )(
        x_rows.reshape(SLOTS, width), g_rows.reshape(SLOTS, width), expert_all, up_bias, vec, cols,
        jnp.swapaxes(gates, 1, 2),
    )

    message = jnp.pad(
        jnp.stack(
            [
                jnp.pad(up_grad.reshape(32, ff_piece), ((0, 0), (0, 128 - ff_piece))),
                jnp.pad(down_grad.reshape(32, piece), ((0, 0), (0, 128 - piece))),
            ],
            axis=1,
        ),
        ((0, 0), (0, 6), (0, 0)),
    )
    e_block, a_block = expert_grad.shape[1:], wall.shape[1:]
    out, token_grad, expert_sum, attn_sum, messages, vec_all = pl.pallas_call(
        functools.partial(back_kernel, cells),
        out_shape=[
            like((rows, width)),
            like((rows, width), F32),
            like(e_block),
            like(a_block[1:], F32),
            like(message.shape, F32),
            like((32, piece, 128), F32),
        ],
        in_specs=[VM] * 11 + [HB, HB],
        out_specs=[VM, VM, HB, VM, HB, VM],
        scratch_shapes=[
            pltpu.VMEM((rows, width), F32),
            pltpu.VMEM((128, width), F32),
            pltpu.VMEM((32, piece, 128), F32),
            pltpu.VMEM(wall.shape, BF),
            pltpu.VMEM((4, 1, 3 * head_cols), F32),
            pltpu.VMEM((2,) + e_block, BF),
            pltpu.VMEM((2,) + a_block, BF),
            pltpu.VMEM((2,) + e_block, BF),
            pltpu.VMEM(e_block, BF),
            pltpu.VMEM(a_block, BF),
            pltpu.VMEM(e_block, BF),
            pltpu.VMEM(a_block, BF),
            pltpu.VMEM(e_block, BF),
            pltpu.VMEM(a_block, BF),
            pltpu.VMEM(a_block, BF),
            dma((2, 2)), dma((2, 2)), dma((2, 8)), dma((2, 8)), dma((2, 8)), dma((2, 8)), dma((4,)),
            dma((31,)), dma((31,)), dma((31,)), dma((31,)),
        ],
        compiler_params=params(2),
        name="back",
    )(tok, hidden, r_rows, m_rows, cot, probs, picked, vec, wall, qkv, mixed, expert_grad, message)

    grads = jnp.sum(vec_all, axis=0).T
    messages = jnp.sum(messages.reshape(8, 4, 8, 128), axis=1)
    up_sum, down_sum = messages[:, 0, :ff_piece], messages[:, 1, :piece]
    if cells > 1:
        expert_sum = lax.psum_scatter(
            expert_sum.astype(F32), "dp", scatter_dimension=2, tiled=True, axis_index_groups=peers
        )
        attn_sum = lax.psum_scatter(attn_sum, "dp", scatter_dimension=0, tiled=True, axis_index_groups=peers)

        def share(part):
            part = lax.psum(part, "dp", axis_index_groups=peers)
            part = lax.all_gather(part, "tensor", axis=1, tiled=True)
            size = part.shape[1] // (4 * cells)
            return lax.dynamic_slice_in_dim(part, (cell * 4 + t) * size, size, 1)

        grads, up_sum, down_sum = share(grads), share(up_sum), share(down_sum)
    return (
        drop_pad(out),
        drop_pad(token_grad),
        grads[0],
        grads[1],
        attn_sum[:, : 3 * head_cols].reshape(-1, 3, head_cols),
        grads[5:7],
        attn_sum[:, 3 * head_cols :].T,
        grads[4],
        grads[2],
        grads[3],
        grads[8:16].T,
        expert_sum[:, 0].astype(F32),
        up_sum,
        jnp.swapaxes(expert_sum[:, 1], 1, 2).astype(F32),
        down_sum,
    )


def solution(mesh):
    both = ("dp", "tensor")
    return jax.shard_map(
        body,
        mesh=mesh,
        in_specs=(
            P(both, None),
            P(both),
            P(both),
            P("dp", None, "tensor"),
            P(None, both),
            P("tensor", "dp"),
            P(both),
            P(both),
            P(both),
            P(both, None),
            P(None, "dp", "tensor"),
            P(None, both),
            P(None, "tensor", "dp"),
            P(None, both),
            P("dp", None),
            P("dp", None),
            P(both, None),
        ),
        out_specs=(
            P(both, None),
            P(both, None),
            P(both),
            P(both),
            P("dp", None, "tensor"),
            P(None, both),
            P("tensor", "dp"),
            P(both),
            P(both),
            P(both),
            P(both, None),
            P(None, "dp", "tensor"),
            P(None, both),
            P(None, "tensor", "dp"),
            P(None, both),
        ),
        check_vma=False,
    )
```

time: 1920 us -> 477 us (0.25)
  waiting for transfers between devices: 851 us -> 0 us
  Pallas kernels: 0 us -> 429 us
  blocking collectives: 358 us -> 0 us
  local copies, waits for them, and re-layouts: 321 us -> 29.2 us
  matrix products: 227 us -> 0 us
  other arithmetic: 118 us -> 8.58 us
  starting transfers between devices: 22.8 us -> 0 us
    reduce_scatter x3 -> x0, waiting for transfers between devices: 704 us -> none  [the longest x1 318 us: body(): lax.psum_scatter(expert_summed[1], 'dp', scatter_dimension=2, tiled=True)]
    pallas_call x0 -> x3, Pallas kernels: none -> 429 us  [the longest x1 184 us: body(): pl.pallas_call(functools.partial(front_kernel, cells), out_shape=[like((r...]
    dot_general x25 -> x0, matrix products: 223 us -> none  [the longest x1 49.7 us: body(): jnp.einsum('ecd,efd->ecf', slot_grad, down_used, preferred_element_type=j...]
    all_gather x6 -> x0, blocking collectives: 206 us -> none  [the longest x1 39.6 us: body(): lax.all_gather(qv_bias, ('dp', 'tensor'), axis=1, tiled=True)]
    unnamed x5 -> x0, blocking collectives: 152 us -> none
    unnamed x20 -> x0, waiting for transfers between devices: 132 us -> none
    reduce_sum x12 -> x2, other arithmetic: 67.5 us -> 0.05 us  [the longest x1 0.04 us: body(): grads = jnp.sum(vec_all, axis=0).T]
    gather x4 -> x0, local copies, waits for them, and re-layouts: 61 us -> none  [the longest x2 30.5 us: body(): back_padded[picks]]
  transfers between devices with their start and end apart: 17 -> 0, of which waited for: 8 -> 0; matrix products, arithmetic and copies ran while one was open for 30% -> 0% of each run, Pallas kernels for 0% -> 0%
where the time goes in v2:
time: 477 us; the launch traced here: 468 us
  Pallas kernels  429 us (90%)
  local copies, waits for them, and re-layouts  29.2 us (6%)
  other arithmetic  8.58 us (2%)
    pallas_call x1, Pallas kernels, body(): pl.pallas_call(functools.partial(front_kernel, cells), out_shape=[like((r...  184 us
    pallas_call x1, Pallas kernels, body(): pl.pallas_call(functools.partial(middle_kernel, cells), out_shape=[like((...  127 us
    pallas_call x1, Pallas kernels, body(): pl.pallas_call(functools.partial(back_kernel, cells), out_shape=[like((ro...  118 us

profile of v2, /device:TPU:11, one launch (start us, length us, event | category | flops | bytes accessed | tf_op | source)
XLA Modules:
  0.0 467.6 jit_solution(14886959044851669098)
XLA Ops:
  1.4 0.8 constant_dynamic-slice_fusion
  2.3 1.3 pad.48.small_b
  3.8 0.7 copy.93
  4.6 0.7 copy.94
  5.3 0.7 copy.97
  6.1 0.7 copy.95
  6.8 0.7 copy.96
  7.6 0.8 copy.100
  8.3 0.8 copy.92
  10.4 0.7 and_select_fusion
  11.2 0.9 copy.90
  12.1 1.1 copy.89
  13.4 0.8 pad_maximum_fusion.1.packed
  14.1 1.2 reshape.93
  15.3 0.9 pad.45
  16.3 0.9 pad.49
  17.6 1.0 fusion
  18.7 0.9 copy.102.cols
  19.6 1.6 pad_maximum_fusion.expert
  21.2 184.4 %front.1 = (f32[416,768]{1,0:T(8,128)}, f32[8,416]{1,0:T(8,128)}, f32[4,8,416]{2,1,0:T(8,128)}, bf16[4,416,576]{2,1,0:T(8,128)(2,1)}, bf16[4,416,192]{2,1,0:T(8,...) custom-call(bf16[96,768]{1,0:T(8,128)(2,1)} %pad_maximum_fusion.1.pa, ...), custom_call_target="tpu_custom_call" | custom-call | tf_op jit(solution)/shard_map/front/pallas_call | solution.py:791
  205.6 0.9 dynamic-slice_bitcast_fusion
  207.2 2.0 copy.104
  209.3 126.6 %middle.1 = (f32[416,768]{1,0:T(8,128)}, f32[416,768]{1,0:T(8,128)}, f32[8,416]{1,0:T(8,128)}, bf16[4,8,2,96,768]{4,3,2,1,0:T(8,128)(2,1)}, f32[4,1,768]{2,1,0:T(1,128)}, /*index=5*/f32[1,768]{1,0:T(1,128)}) custom-call(bf16[1280,768]{1,0:T(8,128)(2,1)} %bitcast.64, bf16[1280,768]{1,0:T(8,128)(2,1)} %bitcast.65, ...), custom_call_target="tpu_custom_call" | custom-call | tf_op jit(solution)/shard_map/middle/pallas_call | solution.py:828
  336.6 0.7 reduce
  338.2 117.7 %back.1 = (bf16[416,768]{1,0:T(8,128)(2,1)}, f32[416,768]{1,0:T(8,128)}, bf16[8,2,96,768]{3,2,1,0:T(8,128)(2,1)}, f32[96,768]{1,0:T(8,128)}, f32[32,8,128]{2,1,0:T(8,128)}, /*index=5*/f32[32,24,128]{2,1,0:T(8,128)}) custom-call(bf16[416,768]{1,0:T(8,128)(2,1)} %bitcast.59, f32[416,768]{1,0:T(8,128)} %get-tuple-element.38.hid, ...), custom_call_target="tpu_custom_call" | custom-call | tf_op jit(solution)/shard_map/back/pallas_call | solution.py:883
  455.9 1.2 slice.73
  457.2 0.9 reshape.108
  458.2 1.1 reshape.110
  459.4 0.8 slice_reduce_fusion
  463.0 0.7 copy.108
  463.8 0.9 copy.106
  464.7 2.7 convert_bitcast_fusion
  (52 shorter events, 8.5 us)
Async XLA Ops:
  0.6 15.6 %copy-start.4 = (bf16[394,768]{1,0:T(8,128)(2,1)S(1)}, bf16[394,768]{1,0:T(8,128)(2,1)}, u32[]{:S(2)}) copy-start(bf16[394,768]{1,0:T(8,128)(2,1)} %param.33) | copy-start | bytes 1815556
  17.6 2.0 copy-start.2
  17.6 2.0 copy-start.3
  455.9 2.2 copy-start.1
  458.1 1.2 copy-start.6
  458.1 3.5 copy-start.7
  458.2 4.6 copy-start.5
  459.4 5.4 %copy-start = (bf16[8,2,96,768]{3,2,1,0:T(8,128)(2,1)S(1)}, bf16[8,2,96,768]{3,2,1,0:T(8,128)(2,1)}, u32[]{:S(2)}) copy-start(bf16[8,2,96,768]{3,2,1,0:T(8,128)(2,1)} %get-tuple-element.59) | copy-start | bytes 7077892
